TPU v7x, 32 devices: a whole 2x2x4 slice. The times are simulated.
32 devices in a mesh: lon: 2 (over x), lat: 4 (over z), lev: 4 (over y, core).
Axes of the slice: x: 2, y: 2, z: 4, core: 2. Of those that a mesh axis runs over, the one named last changes fastest.
Arguments:
- solution: float32 [36, 8, 32, 256], P(None, 'lev', 'lat', 'lon'), may hold values from -6 to 6
- residual: float32 [36, 8, 32, 256], P(None, 'lev', 'lat', 'lon'), may hold values from -24 to 24
- direction: float32 [36, 8, 32, 256], P(None, 'lev', 'lat', 'lon'), may hold values from -24 to 24
- ensemble: bfloat16 [32, 4, 8, 32, 256], P(None, None, 'lev', 'lat', 'lon'), may hold values from -6 to 6
- static_sd: float32 [4, 8, 32, 256], P(None, 'lev', 'lat', 'lon'), may hold values from 0.5 to 2
- send_tile: int32 [4, 2, 4, 8, 2], P('lev', 'lon', 'lat'), may hold values from 0 to 15
- pair_count: int32 [4, 2, 4, 8], P('lev', 'lon', 'lat'), may hold values from 1 to 2, as said below
- obs_weight: bfloat16 [4, 2, 4, 8, 2, 8, 512], P('lev', 'lon', 'lat'), may hold values from -0.25 to 0.25
- obs_precision: float32 [4, 2, 4, 8, 2, 8], P('lev', 'lon', 'lat'), may hold values from 100 to 3000
Outputs:
- new_solution: float32 [36, 8, 32, 256], P(None, 'lev', 'lat', 'lon')
- new_residual: float32 [36, 8, 32, 256], P(None, 'lev', 'lat', 'lon')
- new_direction: float32 [36, 8, 32, 256], P(None, 'lev', 'lat', 'lon')
Inputs may be any that keep to these rules, and one draw needn't show every extreme that they name: `pair_count`: every device sends at least one and at most 2 live slots to every owner of its level plane; in every level plane some owner has 2 live slots from every device of the plane.
All inputs are finite; a program needn't handle non-finite values.
Results may differ from a plain program's by a relative error of at most 0.0034.
Values may be sent and summed in bfloat16 or wider, within the bound.
A program may use at most 64 MiB of HBM per device.

v0:
```python
import jax
import jax.numpy as jnp
from jax import lax
from jax.sharding import PartitionSpec as P

spread_lon = 0.075
spread_lat = 0.3
spread_lev = 0.075
ens_share = 0.75
static_part = 0.5


def with_halo(block, sides, width):
    for axis, dim in sides:
        count = lax.axis_size(axis)
        forward = [(i, i + 1) for i in range(count - 1)]
        forward.append((count - 1, 0))
        backward = [(target, source) for source, target in forward]
        low = lax.ppermute(
            lax.slice_in_dim(block, block.shape[dim] - width, None, axis=dim), axis, forward
        )
        high = lax.ppermute(lax.slice_in_dim(block, 0, width, axis=dim), axis, backward)
        block = jnp.concatenate([low, block, high], axis=dim)
    return block


def one_pass(padded):
    centre = padded[:, 1:-1, 1:-1, 1:-1]
    result = centre * (1.0 - 2.0 * (spread_lon + spread_lat + spread_lev))
    result = result + spread_lon * (padded[:, 1:-1, 1:-1, 2:] + padded[:, 1:-1, 1:-1, :-2])
    result = result + spread_lat * (padded[:, 1:-1, 2:, 1:-1] + padded[:, 1:-1, :-2, 1:-1])
    result = result + spread_lev * (padded[:, 2:, 1:-1, 1:-1] + padded[:, :-2, 1:-1, 1:-1])
    return result


def inside_mask(levels, lat_rows, margin):
    lev_first = lax.axis_index("lev") * levels - margin
    lat_first = lax.axis_index("lat") * lat_rows - margin
    lev_total = levels * lax.axis_size("lev")
    lat_total = lat_rows * lax.axis_size("lat")
    lev_where = lev_first + jnp.arange(levels + 2 * margin, dtype=jnp.int32)
    lat_where = lat_first + jnp.arange(lat_rows + 2 * margin, dtype=jnp.int32)
    lev_inside = (lev_where >= 0) & (lev_where < lev_total)
    lat_inside = (lat_where >= 0) & (lat_where < lat_total)
    return (lev_inside[:, None] & lat_inside[None, :]).astype(jnp.float32)[:, :, None]


def smooth(fields):
    levels, lat_rows = (fields.shape[1], fields.shape[2])
    inside = inside_mask(levels, lat_rows, 2)
    for pass_index in range(2):
        padded = with_halo(fields, (("lon", 3), ("lat", 2), ("lev", 1)), 2)
        fields = one_pass(padded * inside) * inside[1:-1, 1:-1]
        fields = one_pass(fields)
    return fields


def body(
    solution,
    residual,
    direction,
    ensemble,
    static_sd,
    send_tile,
    pair_count,
    obs_weight,
    obs_precision,
):
    members, variables, levels, lat_rows, lon_cells = ensemble.shape
    scale_ens = (ens_share / members) ** 0.5
    tile_width = variables * lon_cells
    tile_total = levels * lat_rows
    group_size = send_tile.shape[3]
    slot_count = send_tile.shape[4]
    obs_count = obs_weight.shape[5]
    start_norm = lax.psum(jnp.sum(residual * residual), ("lon", "lat", "lev"))
    smoothed = smooth(direction)
    ens_part = jnp.sum(ensemble * smoothed[:members, None], axis=0)
    increment = (scale_ens * ens_part + static_part * static_sd * smoothed[members:]).astype(
        jnp.bfloat16
    )
    tile_table = increment.transpose(1, 2, 0, 3).reshape(tile_total, tile_width)
    tile_pick = send_tile.reshape(group_size * slot_count)
    is_live = (
        jnp.arange(slot_count, dtype=jnp.int32)[None, :] < pair_count.reshape(group_size)[:, None]
    )
    outgoing = jnp.take(tile_table, tile_pick, axis=0)
    outgoing = jnp.where(
        is_live.reshape(group_size * slot_count)[:, None], outgoing, jnp.zeros_like(outgoing)
    )
    outgoing = outgoing.reshape(group_size, slot_count, tile_width)
    arrived = lax.all_to_all(outgoing, ("lon", "lat"), split_axis=0, concat_axis=0, tiled=True)
    weights = obs_weight.reshape(group_size, slot_count, obs_count, tile_width)
    predicted = jnp.einsum("gsbc,gsc->gsb", weights, arrived, preferred_element_type=jnp.float32)
    weighted = (obs_precision.reshape(group_size, slot_count, obs_count) * predicted).astype(
        jnp.bfloat16
    )
    returned = jnp.einsum("gsbc,gsb->gsc", weights, weighted, preferred_element_type=jnp.float32)
    came_back = lax.all_to_all(returned, ("lon", "lat"), split_axis=0, concat_axis=0, tiled=True)
    came_back = came_back.reshape(group_size * slot_count, tile_width)
    one_hot = (tile_pick[:, None] == jnp.arange(tile_total, dtype=jnp.int32)[None, :]).astype(
        jnp.float32
    )
    adj_tiles = jnp.dot(
        one_hot.T, came_back, precision=lax.Precision.HIGHEST, preferred_element_type=jnp.float32
    )
    adjoint = adj_tiles.reshape(levels, lat_rows, variables, lon_cells).transpose(2, 0, 1, 3)
    back_ens = scale_ens * jnp.sum(ensemble * adjoint[None], axis=1)
    back_static = static_part * static_sd * adjoint
    back = jnp.concatenate([back_ens, back_static], axis=0)
    image_field = direction + smooth(back)
    curvature = lax.psum(jnp.sum(direction * image_field), ("lon", "lat", "lev"))
    step_size = start_norm / curvature
    new_residual = residual - step_size * image_field
    next_norm = lax.psum(jnp.sum(new_residual * new_residual), ("lon", "lat", "lev"))
    new_solution = solution + step_size * direction
    new_direction = new_residual + next_norm / (start_norm + 1e-06) * direction
    return (new_solution, new_residual, new_direction)


def solution(mesh):
    in_specs = (
        P(None, "lev", "lat", "lon"),
        P(None, "lev", "lat", "lon"),
        P(None, "lev", "lat", "lon"),
        P(None, None, "lev", "lat", "lon"),
        P(None, "lev", "lat", "lon"),
        P("lev", "lon", "lat", None, None),
        P("lev", "lon", "lat", None),
        P("lev", "lon", "lat", None, None, None, None),
        P("lev", "lon", "lat", None, None, None),
    )
    out_specs = (
        P(None, "lev", "lat", "lon"),
        P(None, "lev", "lat", "lon"),
        P(None, "lev", "lat", "lon"),
    )
    return jax.shard_map(body, mesh=mesh, in_specs=in_specs, out_specs=out_specs, check_vma=False)
```

profile of v0, /device:TPU:0, one launch (start us, length us, event | category | flops | bytes accessed | tf_op | source)
XLA Modules:
  0.0 326.6 jit_solution(8138992434252728498)
XLA Ops:
  0.7 1.2 fusion.76
  1.9 3.0 collective-permute-start
  5.0 7.7 %collective-permute-done = f32[36,2,8,2]{3,2,0,1:T(8,128)S(1)} collective-permute-done((f32[36,2,8,2]{3,2,0,1:T(8,128)S(1)}, f32[36,2,8,2]{3,2,0,1:T(8,128)S(1)}, u32[]{:S(2)}, u32[]{:S(2)}) %collective-permute-start) | collective-permute-done | bytes 4640 | tf_op jit(solution)/shard_map/ppermute | solution.py:19
  12.7 5.5 %collective-permute-done.1 = f32[36,2,8,2]{3,2,0,1:T(8,128)S(1)} collective-permute-done((f32[36,2,8,2]{3,2,0,1:T(8,128)S(1)}, f32[36,2,8,2]{3,2,0,1:T(8,128)S(1)}, u32[]{:S(2)}, u32[]{:S(2)}) %collective-permute-start.1) | collective-permute-done | bytes 4640 | tf_op jit(solution)/shard_map/ppermute | solution.py:22
  18.2 1.6 pad_maximum_fusion.17
  19.8 1.9 collective-permute-start.2
  21.7 2.1 collective-permute-start.3
  23.8 4.5 %collective-permute-done.2 = f32[36,2,2,132]{3,2,0,1:T(2,128)S(1)} collective-permute-done((f32[36,2,2,132]{3,2,0,1:T(2,128)S(1)}, f32[36,2,2,132]{3,2,0,1:T(2,128)S(1)}, u32[]{:S(2)}, u32[]{:S(2)}) %collective-permute-start.2) | collective-permute-done | bytes 76064 | tf_op jit(solution)/shard_map/ppermute | solution.py:19
  28.3 1.0 collective-permute-done.3
  29.9 0.7 copy.57
  30.7 1.7 collective-permute-start.5
  32.6 18.1 %collective-permute-done.4 = f32[36,2,12,132]{3,1,2,0:T(2,128)S(1)} collective-permute-done((f32[36,2,12,132]{3,1,2,0:T(2,128)S(1)}, f32[36,2,12,132]{3,1,2,0:T(2,128)S(1)}, u32[]{:S(2)}, u32[]{:S(2)}) %collective-permute-start.4) | collective-permute-done | bytes 456224 | tf_op jit(solution)/shard_map/ppermute | solution.py:19
  50.9 0.8 collective-permute-done.5
  51.8 1.1 maximum_multiply_fusion
  52.9 3.8 %fusion.23 = f32[36,4,10,130]{3,2,0,1:T(8,128)S(1)} fusion(f32[36,6,12,132]{3,2,0,1:T(8,128)S(1)} %maximum_multiply_fusion, f32[4,10]{1,0:T(4,128)S(1)} %convert_bitcast_fusion), kind=kLoop, calls=%fused_computation.41 | loop fusion | flops 2059200 | bytes 5990560 | tf_op jit(solution)/shard_map/mul | solution.py:53
  57.4 1.6 collective-permute-start.6
  59.5 7.9 %collective-permute-done.6 = f32[36,2,8,2]{3,2,0,1:T(8,128)S(1)} collective-permute-done((f32[36,2,8,2]{3,2,0,1:T(8,128)S(1)}, f32[36,2,8,2]{3,2,0,1:T(8,128)S(1)}, u32[]{:S(2)}, u32[]{:S(2)}) %collective-permute-start.6) | collective-permute-done | bytes 4640 | tf_op jit(solution)/shard_map/ppermute | solution.py:19
  67.4 6.1 %collective-permute-done.7 = f32[36,2,8,2]{3,2,0,1:T(8,128)S(1)} collective-permute-done((f32[36,2,8,2]{3,2,0,1:T(8,128)S(1)}, f32[36,2,8,2]{3,2,0,1:T(8,128)S(1)}, u32[]{:S(2)}, u32[]{:S(2)}) %collective-permute-start.7) | collective-permute-done | bytes 4640 | tf_op jit(solution)/shard_map/ppermute | solution.py:22
  74.1 1.2 collective-permute-start.8
  75.3 2.7 collective-permute-start.9
  78.2 4.4 %collective-permute-done.8 = f32[36,2,2,132]{3,2,0,1:T(2,128)S(1)} collective-permute-done((f32[36,2,2,132]{3,2,0,1:T(2,128)S(1)}, f32[36,2,2,132]{3,2,0,1:T(2,128)S(1)}, u32[]{:S(2)}, u32[]{:S(2)}) %collective-permute-start.8) | collective-permute-done | bytes 76064 | tf_op jit(solution)/shard_map/ppermute | solution.py:19
  82.6 1.2 collective-permute-done.9
  84.4 0.7 copy.61
  85.2 1.7 collective-permute-start.11
  87.0 18.5 %collective-permute-done.10 = f32[36,2,12,132]{3,1,2,0:T(2,128)S(1)} collective-permute-done((f32[36,2,12,132]{3,1,2,0:T(2,128)S(1)}, f32[36,2,12,132]{3,1,2,0:T(2,128)S(1)}, u32[]{:S(2)}, u32[]{:S(2)}) %collective-permute-start.10) | collective-permute-done | bytes 456224 | tf_op jit(solution)/shard_map/ppermute | solution.py:19
  106.0 1.1 maximum_multiply_fusion.1
  107.1 3.8 %fusion.16 = f32[36,4,10,130]{3,2,0,1:T(8,128)S(1)} fusion(f32[36,6,12,132]{3,2,0,1:T(8,128)S(1)} %maximum_multiply_fusion.1, f32[4,10]{1,0:T(4,128)S(1)} %convert_bitcast_fusion), kind=kLoop, calls=%fused_computation.30 | loop fusion | flops 2059200 | bytes 5990560 | tf_op jit(solution)/shard_map/mul | solution.py:53
  112.8 0.7 broadcast_select_fusion.1
  113.5 4.3 %all-to-all-start = ((bf16[8,2,512]{2,1,0:T(2,128)(2,1)}), bf16[8,2,512]{2,1,0:T(2,128)(2,1)S(1)}, u32[]{:S(2)}, u32[]{:S(2)}) async-start(bf16[8,2,512]{2,1,0:T(2,128)(2,1)} %broadcast_select_fusion.1), calls=%async_computation | async-start | bytes 32768 | tf_op jit(solution)/shard_map/all_to_all | solution.py:92
  117.8 6.5 %all-to-all-done = bf16[8,2,512]{2,1,0:T(2,128)(2,1)S(1)} async-done(((bf16[8,2,512]{2,1,0:T(2,128)(2,1)}), bf16[8,2,512]{2,1,0:T(2,128)(2,1)S(1)}, u32[]{:S(2)}, u32[]{:S(2)}) %all-to-all-start) | async-done | bytes 16416 | tf_op jit(solution)/shard_map/all_to_all | solution.py:92
  124.7 0.6 copy.145
  125.4 3.3 %all-to-all-start.1 = ((f32[8,2,512]{2,1,0:T(2,128)}), f32[8,2,512]{2,1,0:T(2,128)S(1)}, u32[]{:S(2)}, u32[]{:S(2)}) async-start(f32[8,2,512]{2,1,0:T(2,128)} %bitcast.59), calls=%async_computation.1 | async-start | bytes 65536 | tf_op jit(solution)/shard_map/all_to_all | solution.py:99
  128.7 6.7 %all-to-all-done.1 = f32[8,2,512]{2,1,0:T(2,128)S(1)} async-done(((f32[8,2,512]{2,1,0:T(2,128)}), f32[8,2,512]{2,1,0:T(2,128)S(1)}, u32[]{:S(2)}, u32[]{:S(2)}) %all-to-all-start.1) | async-done | bytes 32800 | tf_op jit(solution)/shard_map/all_to_all | solution.py:99
  135.9 0.6 collective-permute-start.12
  136.5 1.5 collective-permute-start.13
  138.0 7.9 %collective-permute-done.12 = f32[36,2,8,2]{3,2,0,1:T(8,128)S(1)} collective-permute-done((f32[36,2,8,2]{3,2,0,1:T(8,128)S(1)}, f32[36,2,8,2]{3,2,0,1:T(8,128)S(1)}, u32[]{:S(2)}, u32[]{:S(2)}) %collective-permute-start.12) | collective-permute-done | bytes 4640 | tf_op jit(solution)/shard_map/ppermute | solution.py:19
  145.9 3.8 %collective-permute-done.13 = f32[36,2,8,2]{3,2,0,1:T(8,128)S(1)} collective-permute-done((f32[36,2,8,2]{3,2,0,1:T(8,128)S(1)}, f32[36,2,8,2]{3,2,0,1:T(8,128)S(1)}, u32[]{:S(2)}, u32[]{:S(2)}) %collective-permute-start.13) | collective-permute-done | bytes 4640 | tf_op jit(solution)/shard_map/ppermute | solution.py:22
  150.7 3.3 %collective-permute-start.15 = (f32[36,2,2,132]{3,2,0,1:T(2,128)S(1)}, f32[36,2,2,132]{3,2,0,1:T(2,128)S(1)}, u32[]{:S(2)}, u32[]{:S(2)}) collective-permute-start(f32[36,2,2,132]{3,2,0,1:T(2,128)S(1)} %get-tuple-element.21), channel_id=1, source_target_pairs={{4,0},{8,4},{12,8},{0,12},{5,1},{9,5},{13,9},{1,13},{6,2},{10,6},{... | collective-permute-start | bytes 228104 | tf_op jit(solution)/shard_map/ppermute | solution.py:22
  154.1 3.3 %collective-permute-done.14 = f32[36,2,2,132]{3,2,0,1:T(2,128)S(1)} collective-permute-done((f32[36,2,2,132]{3,2,0,1:T(2,128)S(1)}, f32[36,2,2,132]{3,2,0,1:T(2,128)S(1)}, u32[]{:S(2)}, u32[]{:S(2)}) %collective-permute-start.14) | collective-permute-done | bytes 76064 | tf_op jit(solution)/shard_map/ppermute | solution.py:19
  158.0 0.7 copy.72
  158.8 1.7 collective-permute-start.17
  160.6 18.6 %collective-permute-done.16 = f32[36,2,12,132]{3,1,2,0:T(2,128)S(1)} collective-permute-done((f32[36,2,12,132]{3,1,2,0:T(2,128)S(1)}, f32[36,2,12,132]{3,1,2,0:T(2,128)S(1)}, u32[]{:S(2)}, u32[]{:S(2)}) %collective-permute-start.16) | collective-permute-done | bytes 456224 | tf_op jit(solution)/shard_map/ppermute | solution.py:19
  179.7 1.5 maximum_multiply_fusion.2
  181.2 3.8 %fusion.9 = f32[36,4,10,130]{3,2,0,1:T(8,128)S(1)} fusion(f32[36,6,12,132]{3,2,0,1:T(8,128)S(1)} %maximum_multiply_fusion.2, f32[4,10]{1,0:T(4,128)S(1)} %convert_bitcast_fusion), kind=kLoop, calls=%fused_computation.19 | loop fusion | flops 2059200 | bytes 5990560 | tf_op jit(solution)/shard_map/mul | solution.py:53
  185.8 0.6 collective-permute-start.18
  186.4 1.5 collective-permute-start.19
  187.8 7.8 %collective-permute-done.18 = f32[36,2,8,2]{3,2,0,1:T(8,128)S(1)} collective-permute-done((f32[36,2,8,2]{3,2,0,1:T(8,128)S(1)}, f32[36,2,8,2]{3,2,0,1:T(8,128)S(1)}, u32[]{:S(2)}, u32[]{:S(2)}) %collective-permute-start.18) | collective-permute-done | bytes 4640 | tf_op jit(solution)/shard_map/ppermute | solution.py:19
  195.6 6.3 %collective-permute-done.19 = f32[36,2,8,2]{3,2,0,1:T(8,128)S(1)} collective-permute-done((f32[36,2,8,2]{3,2,0,1:T(8,128)S(1)}, f32[36,2,8,2]{3,2,0,1:T(8,128)S(1)}, u32[]{:S(2)}, u32[]{:S(2)}) %collective-permute-start.19) | collective-permute-done | bytes 4640 | tf_op jit(solution)/shard_map/ppermute | solution.py:22
  203.0 3.4 %collective-permute-start.21 = (f32[36,2,2,132]{3,2,0,1:T(2,128)S(1)}, f32[36,2,2,132]{3,2,0,1:T(2,128)S(1)}, u32[]{:S(2)}, u32[]{:S(2)}) collective-permute-start(f32[36,2,2,132]{3,2,0,1:T(2,128)S(1)} %get-tuple-element.19), channel_id=1, source_target_pairs={{4,0},{8,4},{12,8},{0,12},{5,1},{9,5},{13,9},{1,13},{6,2},{10,6},{... | collective-permute-start | bytes 228104 | tf_op jit(solution)/shard_map/ppermute | solution.py:22
  206.4 4.7 %collective-permute-done.20 = f32[36,2,2,132]{3,2,0,1:T(2,128)S(1)} collective-permute-done((f32[36,2,2,132]{3,2,0,1:T(2,128)S(1)}, f32[36,2,2,132]{3,2,0,1:T(2,128)S(1)}, u32[]{:S(2)}, u32[]{:S(2)}) %collective-permute-start.20) | collective-permute-done | bytes 76064 | tf_op jit(solution)/shard_map/ppermute | solution.py:19
  211.1 1.0 collective-permute-done.21
  212.6 0.7 copy.76
  213.4 1.7 collective-permute-start.23
  215.1 0.7 multiply_reduce_fusion.2
  215.8 18.0 %collective-permute-done.22 = f32[36,2,12,132]{3,1,2,0:T(2,128)S(1)} collective-permute-done((f32[36,2,12,132]{3,1,2,0:T(2,128)S(1)}, f32[36,2,12,132]{3,1,2,0:T(2,128)S(1)}, u32[]{:S(2)}, u32[]{:S(2)}) %collective-permute-start.22) | collective-permute-done | bytes 456224 | tf_op jit(solution)/shard_map/ppermute | solution.py:19
  234.2 1.1 maximum_multiply_fusion.3
  235.3 3.8 %fusion.2 = f32[36,4,10,130]{3,2,0,1:T(8,128)S(1)} fusion(f32[36,6,12,132]{3,2,0,1:T(8,128)S(1)} %maximum_multiply_fusion.3, f32[4,10]{1,0:T(4,128)S(1)} %convert_bitcast_fusion), kind=kLoop, calls=%fused_computation.8 | loop fusion | flops 2059200 | bytes 5990560 | tf_op jit(solution)/shard_map/mul | solution.py:53
  239.2 1.1 multiply_reduce_fusion.1
  240.3 40.1 %all-reduce = (f32[]{:T(128)}, f32[]{:T(128)}) all-reduce(f32[]{:T(128)} %multiply_reduce_fusion.2, f32[]{:T(128)} %get-tuple-element.16), channel_id=1, replica_groups=mesh['lon'=2,'lat'=4,'lev'=4] {'lon','lat','lev'}, use_global_device_ids=true, to_apply=%region_1.0 | all-reduce | flops 2 | bytes 16 | tf_op jit(solution)/shard_map/psum | solution.py:76
  281.8 0.7 multiply_reduce_fusion
  282.5 40.5 %psum.23 = f32[]{:T(128)} all-reduce(f32[]{:T(128)} %get-tuple-element.14), channel_id=1, replica_groups=mesh['lon'=2,'lat'=4,'lev'=4] {'lon','lat','lev'}, use_global_device_ids=true, to_apply=%region_7.8 | all-reduce | flops 1 | bytes 8 | tf_op jit(solution)/shard_map/psum | solution.py:115
  323.6 0.7 copy.87
  325.1 0.7 copy.86
  325.8 0.7 copy.88
  (77 shorter events, 12.2 us)
Async XLA Ops:
  0.6 123.7 %copy-start = (bf16[1,1,1,8,2,8,512]{6,5,4,3,2,1,0:T(8,128)(2,1)S(1)}, bf16[1,1,1,8,2,8,512]{6,5,4,3,2,1,0:T(8,128)(2,1)}, u32[]{:S(2)}) copy-start(bf16[1,1,1,8,2,8,512]{6,5,4,3,2,1,0:T(8,128)(2,1)} %param.16) | copy-start | bytes 393220
  0.6 28.7 %copy-start.1 = (f32[36,2,8,128]{3,2,1,0:T(8,128)S(1)}, f32[36,2,8,128]{3,2,1,0:T(8,128)}, u32[]{:S(2)}) copy-start(f32[36,2,8,128]{3,2,1,0:T(8,128)} %param.11) | copy-start | bytes 884740
  1.9 10.8 %collective-permute-start = (f32[36,2,8,2]{3,2,0,1:T(8,128)S(1)}, f32[36,2,8,2]{3,2,0,1:T(8,128)S(1)}, u32[]{:S(2)}, u32[]{:S(2)}) collective-permute-start(f32[36,2,8,2]{3,2,0,1:T(8,128)S(1)} %get-tuple-element.34), channel_id=1, source_target_pairs={{0,16},{16,0},{1,17},{17,1},{2,18},{18,2},{3,19},{19,3},{4,20},{20... | collective-permute-start | bytes 13832 | tf_op jit(solution)/shard_map/ppermute | solution.py:19
  4.9 13.3 %collective-permute-start.1 = (f32[36,2,8,2]{3,2,0,1:T(8,128)S(1)}, f32[36,2,8,2]{3,2,0,1:T(8,128)S(1)}, u32[]{:S(2)}, u32[]{:S(2)}) collective-permute-start(f32[36,2,8,2]{3,2,0,1:T(8,128)S(1)} %get-tuple-element.35), channel_id=1, source_target_pairs={{16,0},{0,16},{17,1},{1,17},{18,2},{2,18},{19,3},{3,19},{20,4},{4,... | collective-permute-start | bytes 13832 | tf_op jit(solution)/shard_map/ppermute | solution.py:22
  19.8 8.5 %collective-permute-start.2 = (f32[36,2,2,132]{3,2,0,1:T(2,128)S(1)}, f32[36,2,2,132]{3,2,0,1:T(2,128)S(1)}, u32[]{:S(2)}, u32[]{:S(2)}) collective-permute-start(f32[36,2,2,132]{3,2,0,1:T(2,128)S(1)} %get-tuple-element.24), channel_id=1, source_target_pairs={{0,4},{4,8},{8,12},{12,0},{1,5},{5,9},{9,13},{13,1},{2,6},{6,10},{... | collective-permute-start | bytes 228104 | tf_op jit(solution)/shard_map/ppermute | solution.py:19
  21.7 7.6 %collective-permute-start.3 = (f32[36,2,2,132]{3,2,0,1:T(2,128)S(1)}, f32[36,2,2,132]{3,2,0,1:T(2,128)S(1)}, u32[]{:S(2)}, u32[]{:S(2)}) collective-permute-start(f32[36,2,2,132]{3,2,0,1:T(2,128)S(1)} %get-tuple-element.25), channel_id=1, source_target_pairs={{4,0},{8,4},{12,8},{0,12},{5,1},{9,5},{13,9},{1,13},{6,2},{10,6},{... | collective-permute-start | bytes 228104 | tf_op jit(solution)/shard_map/ppermute | solution.py:22
  30.6 20.1 %collective-permute-start.4 = (f32[36,2,12,132]{3,1,2,0:T(2,128)S(1)}, f32[36,2,12,132]{3,1,2,0:T(2,128)S(1)}, u32[]{:S(2)}, u32[]{:S(2)}) collective-permute-start(f32[36,2,12,132]{3,1,2,0:T(2,128)S(1)} %copy.57), channel_id=1, source_target_pairs={{0,1},{1,2},{2,3},{3,0},{4,5},{5,6},{6,7},{7,4},{8,9},{9,10},{10,1... | collective-permute-start | bytes 1368584 | tf_op jit(solution)/shard_map/ppermute | solution.py:19
  30.7 21.0 %collective-permute-start.5 = (f32[36,2,12,132]{3,1,2,0:T(2,128)S(1)}, f32[36,2,12,132]{3,1,2,0:T(2,128)S(1)}, u32[]{:S(2)}, u32[]{:S(2)}) collective-permute-start(f32[36,2,12,132]{3,1,2,0:T(2,128)S(1)} %copy.57), channel_id=1, source_target_pairs={{1,0},{2,1},{3,2},{0,3},{5,4},{6,5},{7,6},{4,7},{9,8},{10,9},{11,1... | collective-permute-start | bytes 1368584 | tf_op jit(solution)/shard_map/ppermute | solution.py:22
  56.8 21.2 %copy-start.7 = (s32[1,1,1,8,2]{3,4,2,1,0:T(2,128)S(1)}, s32[1,1,1,8,2]{3,4,2,1,0:T(2,128)}, u32[]{:S(2)}) copy-start(s32[1,1,1,8,2]{3,4,2,1,0:T(2,128)} %param.14) | copy-start | bytes 196
  57.4 9.9 %collective-permute-start.6 = (f32[36,2,8,2]{3,2,0,1:T(8,128)S(1)}, f32[36,2,8,2]{3,2,0,1:T(8,128)S(1)}, u32[]{:S(2)}, u32[]{:S(2)}) collective-permute-start(f32[36,2,8,2]{3,2,0,1:T(8,128)S(1)} %get-tuple-element.32), channel_id=1, source_target_pairs={{0,16},{16,0},{1,17},{17,1},{2,18},{18,2},{3,19},{19,3},{4,20},{20... | collective-permute-start | bytes 13832 | tf_op jit(solution)/shard_map/ppermute | solution.py:19
  59.0 14.5 %collective-permute-start.7 = (f32[36,2,8,2]{3,2,0,1:T(8,128)S(1)}, f32[36,2,8,2]{3,2,0,1:T(8,128)S(1)}, u32[]{:S(2)}, u32[]{:S(2)}) collective-permute-start(f32[36,2,8,2]{3,2,0,1:T(8,128)S(1)} %get-tuple-element.33), channel_id=1, source_target_pairs={{16,0},{0,16},{17,1},{1,17},{18,2},{2,18},{19,3},{3,19},{20,4},{4,... | collective-permute-start | bytes 13832 | tf_op jit(solution)/shard_map/ppermute | solution.py:22
  74.1 12.9 %copy-start.8 = (s32[1,1,1,8]{3,2,1,0:T(1,128)S(1)}, s32[1,1,1,8]{3,2,1,0:T(1,128)}, u32[]{:S(2)}) copy-start(s32[1,1,1,8]{3,2,1,0:T(1,128)} %param.15) | copy-start | bytes 100
  74.1 8.6 %collective-permute-start.8 = (f32[36,2,2,132]{3,2,0,1:T(2,128)S(1)}, f32[36,2,2,132]{3,2,0,1:T(2,128)S(1)}, u32[]{:S(2)}, u32[]{:S(2)}) collective-permute-start(f32[36,2,2,132]{3,2,0,1:T(2,128)S(1)} %get-tuple-element.22), channel_id=1, source_target_pairs={{0,4},{4,8},{8,12},{12,0},{1,5},{5,9},{9,13},{13,1},{2,6},{6,10},{... | collective-permute-start | bytes 228104 | tf_op jit(solution)/shard_map/ppermute | solution.py:19
  75.3 8.6 %collective-permute-start.9 = (f32[36,2,2,132]{3,2,0,1:T(2,128)S(1)}, f32[36,2,2,132]{3,2,0,1:T(2,128)S(1)}, u32[]{:S(2)}, u32[]{:S(2)}) collective-permute-start(f32[36,2,2,132]{3,2,0,1:T(2,128)S(1)} %get-tuple-element.23), channel_id=1, source_target_pairs={{4,0},{8,4},{12,8},{0,12},{5,1},{9,5},{13,9},{1,13},{6,2},{10,6},{... | collective-permute-start | bytes 228104 | tf_op jit(solution)/shard_map/ppermute | solution.py:22
  85.1 20.4 %collective-permute-start.10 = (f32[36,2,12,132]{3,1,2,0:T(2,128)S(1)}, f32[36,2,12,132]{3,1,2,0:T(2,128)S(1)}, u32[]{:S(2)}, u32[]{:S(2)}) collective-permute-start(f32[36,2,12,132]{3,1,2,0:T(2,128)S(1)} %copy.61), channel_id=1, source_target_pairs={{0,1},{1,2},{2,3},{3,0},{4,5},{5,6},{6,7},{7,4},{8,9},{9,10},{10,1... | collective-permute-start | bytes 1368584 | tf_op jit(solution)/shard_map/ppermute | solution.py:19
  85.2 20.7 %collective-permute-start.11 = (f32[36,2,12,132]{3,1,2,0:T(2,128)S(1)}, f32[36,2,12,132]{3,1,2,0:T(2,128)S(1)}, u32[]{:S(2)}, u32[]{:S(2)}) collective-permute-start(f32[36,2,12,132]{3,1,2,0:T(2,128)S(1)} %copy.61), channel_id=1, source_target_pairs={{1,0},{2,1},{3,2},{0,3},{5,4},{6,5},{7,6},{4,7},{9,8},{10,9},{11,1... | collective-permute-start | bytes 1368584 | tf_op jit(solution)/shard_map/ppermute | solution.py:22
  111.0 1.0 copy-start.2
  111.0 1.2 copy-start.5
  111.0 13.5 %copy-start.6 = (f32[1,1,1,8,2,8]{5,4,3,2,1,0:T(2,128)S(1)}, f32[1,1,1,8,2,8]{5,4,3,2,1,0:T(2,128)}, u32[]{:S(2)}) copy-start(f32[1,1,1,8,2,8]{5,4,3,2,1,0:T(2,128)} %param.17) | copy-start | bytes 1540
  113.5 10.9 %all-to-all-start = ((bf16[8,2,512]{2,1,0:T(2,128)(2,1)}), bf16[8,2,512]{2,1,0:T(2,128)(2,1)S(1)}, u32[]{:S(2)}, u32[]{:S(2)}) async-start(bf16[8,2,512]{2,1,0:T(2,128)(2,1)} %broadcast_select_fusion.1), calls=%async_computation | async-start | bytes 32768 | tf_op jit(solution)/shard_map/all_to_all | solution.py:92
  125.4 10.0 %all-to-all-start.1 = ((f32[8,2,512]{2,1,0:T(2,128)}), f32[8,2,512]{2,1,0:T(2,128)S(1)}, u32[]{:S(2)}, u32[]{:S(2)}) async-start(f32[8,2,512]{2,1,0:T(2,128)} %bitcast.59), calls=%async_computation.1 | async-start | bytes 65536 | tf_op jit(solution)/shard_map/all_to_all | solution.py:99
  135.9 10.0 %collective-permute-start.12 = (f32[36,2,8,2]{3,2,0,1:T(8,128)S(1)}, f32[36,2,8,2]{3,2,0,1:T(8,128)S(1)}, u32[]{:S(2)}, u32[]{:S(2)}) collective-permute-start(f32[36,2,8,2]{3,2,0,1:T(8,128)S(1)} %get-tuple-element.30), channel_id=1, source_target_pairs={{0,16},{16,0},{1,17},{17,1},{2,18},{18,2},{3,19},{19,3},{4,20},{20... | collective-permute-start | bytes 13832 | tf_op jit(solution)/shard_map/ppermute | solution.py:19
  136.5 13.2 %collective-permute-start.13 = (f32[36,2,8,2]{3,2,0,1:T(8,128)S(1)}, f32[36,2,8,2]{3,2,0,1:T(8,128)S(1)}, u32[]{:S(2)}, u32[]{:S(2)}) collective-permute-start(f32[36,2,8,2]{3,2,0,1:T(8,128)S(1)} %get-tuple-element.31), channel_id=1, source_target_pairs={{16,0},{0,16},{17,1},{1,17},{18,2},{2,18},{19,3},{3,19},{20,4},{4,... | collective-permute-start | bytes 13832 | tf_op jit(solution)/shard_map/ppermute | solution.py:22
  150.2 7.1 %collective-permute-start.14 = (f32[36,2,2,132]{3,2,0,1:T(2,128)S(1)}, f32[36,2,2,132]{3,2,0,1:T(2,128)S(1)}, u32[]{:S(2)}, u32[]{:S(2)}) collective-permute-start(f32[36,2,2,132]{3,2,0,1:T(2,128)S(1)} %get-tuple-element.20), channel_id=1, source_target_pairs={{0,4},{4,8},{8,12},{12,0},{1,5},{5,9},{9,13},{13,1},{2,6},{6,10},{... | collective-permute-start | bytes 228104 | tf_op jit(solution)/shard_map/ppermute | solution.py:19
  150.7 6.7 %collective-permute-start.15 = (f32[36,2,2,132]{3,2,0,1:T(2,128)S(1)}, f32[36,2,2,132]{3,2,0,1:T(2,128)S(1)}, u32[]{:S(2)}, u32[]{:S(2)}) collective-permute-start(f32[36,2,2,132]{3,2,0,1:T(2,128)S(1)} %get-tuple-element.21), channel_id=1, source_target_pairs={{4,0},{8,4},{12,8},{0,12},{5,1},{9,5},{13,9},{1,13},{6,2},{10,6},{... | collective-permute-start | bytes 228104 | tf_op jit(solution)/shard_map/ppermute | solution.py:22
  158.8 20.4 %collective-permute-start.16 = (f32[36,2,12,132]{3,1,2,0:T(2,128)S(1)}, f32[36,2,12,132]{3,1,2,0:T(2,128)S(1)}, u32[]{:S(2)}, u32[]{:S(2)}) collective-permute-start(f32[36,2,12,132]{3,1,2,0:T(2,128)S(1)} %copy.72), channel_id=1, source_target_pairs={{0,1},{1,2},{2,3},{3,0},{4,5},{5,6},{6,7},{7,4},{8,9},{9,10},{10,1... | collective-permute-start | bytes 1368584 | tf_op jit(solution)/shard_map/ppermute | solution.py:19
  158.8 20.7 %collective-permute-start.17 = (f32[36,2,12,132]{3,1,2,0:T(2,128)S(1)}, f32[36,2,12,132]{3,1,2,0:T(2,128)S(1)}, u32[]{:S(2)}, u32[]{:S(2)}) collective-permute-start(f32[36,2,12,132]{3,1,2,0:T(2,128)S(1)} %copy.72), channel_id=1, source_target_pairs={{1,0},{2,1},{3,2},{0,3},{5,4},{6,5},{7,6},{4,7},{9,8},{10,9},{11,1... | collective-permute-start | bytes 1368584 | tf_op jit(solution)/shard_map/ppermute | solution.py:22
  185.8 9.9 %collective-permute-start.18 = (f32[36,2,8,2]{3,2,0,1:T(8,128)S(1)}, f32[36,2,8,2]{3,2,0,1:T(8,128)S(1)}, u32[]{:S(2)}, u32[]{:S(2)}) collective-permute-start(f32[36,2,8,2]{3,2,0,1:T(8,128)S(1)} %get-tuple-element.28), channel_id=1, source_target_pairs={{0,16},{16,0},{1,17},{17,1},{2,18},{18,2},{3,19},{19,3},{4,20},{20... | collective-permute-start | bytes 13832 | tf_op jit(solution)/shard_map/ppermute | solution.py:19
  186.4 15.6 %collective-permute-start.19 = (f32[36,2,8,2]{3,2,0,1:T(8,128)S(1)}, f32[36,2,8,2]{3,2,0,1:T(8,128)S(1)}, u32[]{:S(2)}, u32[]{:S(2)}) collective-permute-start(f32[36,2,8,2]{3,2,0,1:T(8,128)S(1)} %get-tuple-element.29), channel_id=1, source_target_pairs={{16,0},{0,16},{17,1},{1,17},{18,2},{2,18},{19,3},{3,19},{20,4},{4,... | collective-permute-start | bytes 13832 | tf_op jit(solution)/shard_map/ppermute | solution.py:22
  202.5 12.7 %copy-start.3 = (f32[36,2,8,128]{3,2,1,0:T(8,128)S(1)}, f32[36,2,8,128]{3,2,1,0:T(8,128)}, u32[]{:S(2)}) copy-start(f32[36,2,8,128]{3,2,1,0:T(8,128)} %param.10) | copy-start | bytes 884740
  202.5 8.6 %collective-permute-start.20 = (f32[36,2,2,132]{3,2,0,1:T(2,128)S(1)}, f32[36,2,2,132]{3,2,0,1:T(2,128)S(1)}, u32[]{:S(2)}, u32[]{:S(2)}) collective-permute-start(f32[36,2,2,132]{3,2,0,1:T(2,128)S(1)} %get-tuple-element.18), channel_id=1, source_target_pairs={{0,4},{4,8},{8,12},{12,0},{1,5},{5,9},{9,13},{13,1},{2,6},{6,10},{... | collective-permute-start | bytes 228104 | tf_op jit(solution)/shard_map/ppermute | solution.py:19
  203.0 9.0 %collective-permute-start.21 = (f32[36,2,2,132]{3,2,0,1:T(2,128)S(1)}, f32[36,2,2,132]{3,2,0,1:T(2,128)S(1)}, u32[]{:S(2)}, u32[]{:S(2)}) collective-permute-start(f32[36,2,2,132]{3,2,0,1:T(2,128)S(1)} %get-tuple-element.19), channel_id=1, source_target_pairs={{4,0},{8,4},{12,8},{0,12},{5,1},{9,5},{13,9},{1,13},{6,2},{10,6},{... | collective-permute-start | bytes 228104 | tf_op jit(solution)/shard_map/ppermute | solution.py:22
  213.3 20.4 %collective-permute-start.22 = (f32[36,2,12,132]{3,1,2,0:T(2,128)S(1)}, f32[36,2,12,132]{3,1,2,0:T(2,128)S(1)}, u32[]{:S(2)}, u32[]{:S(2)}) collective-permute-start(f32[36,2,12,132]{3,1,2,0:T(2,128)S(1)} %copy.76), channel_id=1, source_target_pairs={{0,1},{1,2},{2,3},{3,0},{4,5},{5,6},{6,7},{7,4},{8,9},{9,10},{10,1... | collective-permute-start | bytes 1368584 | tf_op jit(solution)/shard_map/ppermute | solution.py:19
  213.4 20.7 %collective-permute-start.23 = (f32[36,2,12,132]{3,1,2,0:T(2,128)S(1)}, f32[36,2,12,132]{3,1,2,0:T(2,128)S(1)}, u32[]{:S(2)}, u32[]{:S(2)}) collective-permute-start(f32[36,2,12,132]{3,1,2,0:T(2,128)S(1)} %copy.76), channel_id=1, source_target_pairs={{1,0},{2,1},{3,2},{0,3},{5,4},{6,5},{7,6},{4,7},{9,8},{10,9},{11,1... | collective-permute-start | bytes 1368584 | tf_op jit(solution)/shard_map/ppermute | solution.py:22
  239.2 85.9 %copy-start.4 = (f32[36,2,8,128]{3,2,1,0:T(8,128)S(1)}, f32[36,2,8,128]{3,2,1,0:T(8,128)}, u32[]{:S(2)}) copy-start(f32[36,2,8,128]{3,2,1,0:T(8,128)} %param.9) | copy-start | bytes 884740
where the time goes:
time: 327 us
  waiting for transfers between devices  161 us (49%)
  blocking collectives  80.7 us (25%)
  starting transfers between devices  39.8 us (12%)
  other arithmetic  31.2 us (10%)
  local copies, waits for them, and re-layouts  9.95 us (3%)
  between operations  3.72 us (1%)
    ppermute x12, waiting for transfers between devices, with_halo(): lax.ppermute(lax.slice_in_dim(block, block.shape[dim] - width, None, axis...  121 us
    psum x1, blocking collectives, body(): lax.psum(jnp.sum(new_residual * new_residual), ('lon', 'lat', 'lev'))  40.5 us
    psum x1, blocking collectives, body(): start_norm = lax.psum(jnp.sum(residual * residual), ('lon', 'lat', 'lev'))  40.1 us
    ppermute x12, waiting for transfers between devices, with_halo(): lax.ppermute(lax.slice_in_dim(block, 0, width, axis=dim), axis, backward)  26.2 us
    ppermute x12, starting transfers between devices, with_halo(): lax.ppermute(lax.slice_in_dim(block, 0, width, axis=dim), axis, backward)  22 us
    mul x9, other arithmetic, smooth(): fields = one_pass(padded * inside) * inside[1:-1, 1:-1]  20.3 us
    ppermute x12, starting transfers between devices, with_halo(): lax.ppermute(lax.slice_in_dim(block, block.shape[dim] - width, None, axis...  10.1 us
    all_to_all x1, waiting for transfers between devices, body(): lax.all_to_all(returned, ('lon', 'lat'), split_axis=0, concat_axis=0, til...  6.65 us
  transfers between devices with their start and end apart: 26, of which 26 were waited for; matrix products, arithmetic and copies ran while one was open for 1% of the time, Pallas kernels for 0%

commit v1 on v0

v1 whole, which is shorter than its diff:
```python
import functools

import jax
import jax.numpy as jnp
from jax import lax
from jax.experimental import pallas as pl
from jax.experimental.pallas import tpu as pltpu
from jax.sharding import PartitionSpec as P

spread_lon = 0.075
spread_lat = 0.3
spread_lev = 0.075
ens_share = 0.75
static_part = 0.5
centre_share = 1.0 - 2.0 * (spread_lon + spread_lat + spread_lev)
PASSES = 4
AXES = ("lon", "lat", "lev")
MESH = pl.DeviceIdType.MESH
f32 = jnp.float32
bf16 = jnp.bfloat16


def each(count, step):
    if count <= 32:
        for k in range(count):
            step(k)
    else:
        lax.fori_loop(0, count, lambda k, carry: (step(k), carry)[1], 0)


def kernel(
    sizes,
    direction,
    residual,
    ensemble,
    static_sd,
    obs_weight,
    obs_precision,
    send_tile,
    pair_count,
    image_out,
    scalars_out,
    field_a,
    field_b,
    lev_send,
    lev_recv,
    lat_send,
    lat_recv,
    lon_send,
    lon_recv,
    tiles_out,
    tiles_in,
    ret_out,
    ret_in,
    sum_send,
    sum_plane,
    sum_lev,
    halo_ssem,
    halo_rsem,
    a2a_ssem,
    a2a_rsem,
    plane_ssem,
    plane_rsem,
    col_ssem,
    col_rsem,
):
    n_lon, n_lat, n_lev = sizes
    members, variables, levels, rows, lanes = ensemble.shape
    fields = direction.shape[0]
    blocks = fields * levels
    group = n_lon * n_lat
    slots = send_tile.shape[4]
    tiles = levels * rows
    scale_ens = (ens_share / members) ** 0.5
    at_lon, at_lat, at_lev = (lax.axis_index(a) for a in AXES)
    me = at_lon * n_lat + at_lat

    def plane_id(k):
        peer = lax.rem(me + k, group)
        return peer, {"lon": peer // n_lat, "lat": lax.rem(peer, n_lat)}

    def lev_id(k):
        return {"lev": lax.rem(at_lev + k, n_lev)}

    barrier = pltpu.get_barrier_semaphore()

    def greet_plane(k):
        pl.semaphore_signal(barrier, inc=1, device_id=plane_id(k + 1)[1], device_id_type=MESH)

    def greet_lev(k):
        pl.semaphore_signal(barrier, inc=1, device_id=lev_id(k + 1), device_id_type=MESH)

    each(group - 1, greet_plane)
    each(n_lev - 1, greet_lev)

    buffers = {"lev": (lev_send, lev_recv), "lat": (lat_send, lat_recv), "lon": (lon_send, lon_recv)}
    places = {"lev": (at_lev, n_lev), "lat": (at_lat, n_lat), "lon": (at_lon, n_lon)}

    def halo_copy(p, axis, side):
        src, dst = buffers[axis]
        place, count = places[axis]
        number = AXES.index(axis)
        return pltpu.make_async_remote_copy(
            src_ref=src.at[p, side],
            dst_ref=dst.at[p, 1 - side],
            send_sem=halo_ssem.at[p, number, side],
            recv_sem=halo_rsem.at[p, number, 1 - side],
            device_id={axis: lax.rem(place + (count - 1 if side == 0 else 1), count)},
            device_id_type=MESH,
        )

    def if_there(axis, side, act):
        place, count = places[axis]
        if axis == "lon":
            act()
        else:
            pl.when(place > 0 if side == 0 else place < count - 1)(act)

    lane_of = lax.broadcasted_iota(jnp.int32, (1, rows, lanes), 2)
    row_of = lax.broadcasted_iota(jnp.int32, (1, rows, lanes), 1)
    west = jnp.where(lane_of > 0, spread_lon, 0.0)
    east = jnp.where(lane_of < lanes - 1, spread_lon, 0.0)
    south = jnp.where(row_of > 0, spread_lat, 0.0)
    north = jnp.where(row_of < rows - 1, spread_lat, 0.0)
    edge_row = lax.broadcasted_iota(jnp.int32, (8, lanes), 0)
    edge_lane = lax.broadcasted_iota(jnp.int32, (8, lanes), 1)
    edges = ((edge_row == 0) & (edge_lane == 0)) | ((edge_row == 1) & (edge_lane == lanes - 1))
    edges = edges.astype(bf16)
    lat_pad = lat_send.shape[2] - blocks

    def send_halos(p, src):
        x4 = src[...].reshape(fields, levels, rows, lanes)
        for side, level in ((0, 0), (1, levels - 1)):
            lev_send[p, side] = x4[:, level].reshape(fields * rows, lanes).astype(bf16)
            if_there("lev", side, lambda side=side: halo_copy(p, "lev", side).start())
        for side, row in ((0, 0), (1, rows - 1)):
            edge = src[pl.ds(row, blocks, stride=rows), :]
            if lat_pad:
                edge = jnp.concatenate([edge, jnp.zeros((lat_pad, lanes), f32)], axis=0)
            lat_send[p, side] = edge.astype(bf16)
            if_there("lat", side, lambda side=side: halo_copy(p, "lat", side).start())
        packed = lax.dot_general(
            edges, src[...].astype(bf16), (((1,), (1,)), ((), ())), preferred_element_type=f32
        )
        for side in (0, 1):
            lon_send[p, side] = packed[side : side + 1]
            halo_copy(p, "lon", side).start()

    chunk = max(c for c in range(1, 13) if fields % c == 0)

    def local_part(src, dst):
        for first in range(0, fields, chunk):
            span = pl.ds(first * levels * rows, chunk * levels * rows)
            x = src[span, :].reshape(chunk * levels, rows, lanes)
            y = x * centre_share
            y = y + west * pltpu.roll(x, 1, 2) + east * pltpu.roll(x, lanes - 1, 2)
            y = y + south * pltpu.roll(x, 1, 1) + north * pltpu.roll(x, rows - 1, 1)
            x4 = x.reshape(chunk, levels, rows, lanes)
            if levels > 1:
                none = jnp.zeros((chunk, 1, rows, lanes), f32)
                above = jnp.concatenate([x4[:, 1:], none], axis=1)
                below = jnp.concatenate([none, x4[:, :-1]], axis=1)
                y = y + spread_lev * (above + below).reshape(chunk * levels, rows, lanes)
            dst[span, :] = y.reshape(chunk * levels * rows, lanes)

    def add_halos(p, dst):
        for side in (0, 1):
            halo_copy(p, "lon", 1 - side).wait_recv()
        ends = jnp.concatenate(
            [lon_recv[p, 0], lon_recv[p, 1], jnp.zeros((6, blocks * rows), f32)], axis=0
        )
        spill = lax.dot_general(
            ends.astype(bf16), edges, (((0,), (0,)), ((), ())), preferred_element_type=f32
        )
        dst[...] += spread_lon * spill
        for side, row in ((0, 0), (1, rows - 1)):
            if_there("lat", side, lambda side=side: halo_copy(p, "lat", 1 - side).wait_recv())
            edge = lat_recv[p, side].astype(f32)[:blocks]
            at = pl.ds(row, blocks, stride=rows)
            dst[at, :] = dst[at, :] + spread_lat * edge
        for side in (0, 1):
            if_there("lev", side, lambda side=side: halo_copy(p, "lev", 1 - side).wait_recv())
        low = lev_recv[p, 0].astype(f32).reshape(fields, 1, rows, lanes) * spread_lev
        high = lev_recv[p, 1].astype(f32).reshape(fields, 1, rows, lanes) * spread_lev
        y4 = dst[...].reshape(fields, levels, rows, lanes)
        if levels == 1:
            y4 = y4 + low + high
        else:
            inner = [y4[:, 1:-1]] if levels > 2 else []
            y4 = jnp.concatenate([y4[:, :1] + low, *inner, y4[:, -1:] + high], axis=1)
        dst[...] = y4.reshape(blocks * rows, lanes)

    def smooth(first_pass):
        src, dst = field_a, field_b
        for p in range(first_pass, first_pass + PASSES):
            send_halos(p, src)
            local_part(src, dst)
            add_halos(p, dst)
            src, dst = dst, src
        return src

    field_a[...] = direction[...].reshape(blocks * rows, lanes)
    for side in (0, 1):
        for axis in ("lat", "lev"):
            place, count = places[axis]

            def clear(axis=axis, side=side):
                for p in range(2 * PASSES):
                    ref = buffers[axis][1]
                    ref[p, side] = jnp.zeros(ref.shape[2:], ref.dtype)

            pl.when(place == 0 if side == 0 else place == count - 1)(clear)

    total = slots * group

    def slot_code(i):
        s, d = i // group, i % group
        tile = send_tile[0, 0, 0, d, s]
        return jnp.where(s < pair_count[0, 0, 0, d], tile, -1)

    def fill(dim, shape):
        where_at = lax.broadcasted_iota(jnp.int32, shape, dim)
        step = lambda i, codes: jnp.where(where_at == i, slot_code(i), codes)
        codes = jnp.zeros(shape, jnp.int32)
        if total <= 32:
            for i in range(total):
                codes = step(i, codes)
        else:
            codes = lax.fori_loop(0, total, step, codes)
        return (codes == lax.broadcasted_iota(jnp.int32, shape, 1 - dim)).astype(f32)

    pick = fill(0, (total, tiles)).astype(bf16)
    place_back = fill(1, (tiles, total))

    obs = obs_precision.shape[5]
    eye = (
        lax.broadcasted_iota(jnp.int32, (1, obs, obs), 1)
        == lax.broadcasted_iota(jnp.int32, (1, obs, obs), 2)
    ).astype(f32)
    precision = [
        jnp.sum(obs_precision[0, 0, 0][:, s : s + 1, :] * eye, axis=2, keepdims=True)
        for s in range(slots)
    ]
    d_all = direction[...]
    r_all = residual[...]
    direction_norm = jnp.sum(d_all * d_all)
    residual_norm = jnp.sum(r_all * r_all)

    pl.semaphore_wait(barrier, group - 1 + n_lev - 1)

    smoothed = smooth(0)

    sm4 = smoothed[...].reshape(fields, levels, rows, lanes)
    ens_part = jnp.zeros((variables, levels, rows, lanes), f32)
    for k in range(members):
        ens_part = ens_part + ensemble[k].astype(f32) * sm4[k][None]
    increment = scale_ens * ens_part + static_part * static_sd[...] * sm4[members:]
    increment = increment.astype(bf16).reshape(variables, tiles, lanes)
    table = jnp.concatenate([increment[v] for v in range(variables)], axis=1)
    outgoing = jnp.dot(pick, table, preferred_element_type=f32)
    height = slots * variables
    for s in range(slots):
        for v in range(variables):
            part = outgoing[s * group : (s + 1) * group, v * lanes : (v + 1) * lanes]
            tiles_out[pl.ds(s * variables + v, group, stride=height), :] = part

    def block_of(ref, g):
        return ref.at[pl.ds(pl.multiple_of(g * height, height), height), :]

    def exchange(turn, src, dst):
        def copy(k):
            peer, device = plane_id(k + 1)
            return pltpu.make_async_remote_copy(
                src_ref=block_of(src, peer),
                dst_ref=block_of(dst, me),
                send_sem=a2a_ssem.at[turn, k],
                recv_sem=a2a_rsem.at[turn, k],
                device_id=device,
                device_id_type=MESH,
            )

        return copy

    def own_block(src, dst):
        block_of(dst, me)[...] = block_of(src, me)[...]

    there = exchange(0, tiles_out, tiles_in)
    each(group - 1, lambda k: there(k).start())
    own_block(tiles_out, tiles_in)
    each(group - 1, lambda k: there(k).wait_recv())

    arrived = tiles_in[...].reshape(group, height, lanes)
    fit = jnp.zeros((1, 1), f32)
    for s in range(slots):
        weights = [
            obs_weight[0, 0, 0, :, s, :, v * lanes : (v + 1) * lanes].astype(f32)
            for v in range(variables)
        ]
        product = jnp.zeros((group, obs, lanes), f32)
        for v in range(variables):
            at = s * variables + v
            product = product + weights[v] * arrived[:, at : at + 1, :]
        predicted = jnp.sum(product, axis=2, keepdims=True)
        weighted = (precision[s] * predicted).astype(bf16).astype(f32)
        fit = fit + jnp.sum(jnp.sum(predicted * weighted, axis=0), axis=0, keepdims=True)
        for v in range(variables):
            ret = jnp.sum(weights[v] * weighted, axis=1, keepdims=True)
            ret_out[pl.ds(s * variables + v, group, stride=height), :] = ret.reshape(group, lanes)

    back_again = exchange(1, ret_out, ret_in)
    each(group - 1, lambda k: back_again(k).start())
    own_block(ret_out, ret_in)

    def sum_copies(turn):
        def plane(k):
            return pltpu.make_async_remote_copy(
                src_ref=sum_send.at[turn, 0],
                dst_ref=sum_plane.at[turn, k + 1],
                send_sem=plane_ssem.at[turn, k],
                recv_sem=plane_rsem.at[turn, k],
                device_id=plane_id(k + 1)[1],
                device_id_type=MESH,
            )

        def column(k):
            return pltpu.make_async_remote_copy(
                src_ref=sum_send.at[turn, 1],
                dst_ref=sum_lev.at[turn, k + 1],
                send_sem=col_ssem.at[turn, k],
                recv_sem=col_rsem.at[turn, k],
                device_id=lev_id(k + 1),
                device_id_type=MESH,
            )

        return plane, column

    def sum_begin(turn, values):
        plane, column = sum_copies(turn)
        sum_send[turn, 0] = values
        sum_plane[turn, 0] = values
        each(group - 1, lambda k: plane(k).start())

    def sum_middle(turn):
        plane, column = sum_copies(turn)
        each(group - 1, lambda k: plane(k).wait_recv())
        values = jnp.sum(sum_plane[turn], axis=0)
        sum_send[turn, 1] = values
        sum_lev[turn, 0] = values
        each(n_lev - 1, lambda k: column(k).start())

    def sum_end(turn):
        plane, column = sum_copies(turn)
        each(n_lev - 1, lambda k: column(k).wait_recv())
        return jnp.sum(sum_lev[turn], axis=0)

    row8 = lax.broadcasted_iota(jnp.int32, (8, lanes), 0)
    mine = jnp.where(row8 == 0, residual_norm, jnp.where(row8 == 1, direction_norm, 0.0))
    sum_begin(0, mine + jnp.where(row8 == 2, fit, 0.0))

    each(group - 1, lambda k: back_again(k).wait_recv())
    came = jnp.concatenate(
        [
            jnp.concatenate(
                [
                    ret_in[pl.ds(s * variables + v, group, stride=height), :]
                    for v in range(variables)
                ],
                axis=1,
            )
            for s in range(slots)
        ],
        axis=0,
    )
    adjoint = jnp.dot(
        place_back, came, precision=lax.Precision.HIGHEST, preferred_element_type=f32
    )
    adjoint = jnp.stack(
        [
            adjoint[:, v * lanes : (v + 1) * lanes].reshape(levels, rows, lanes)
            for v in range(variables)
        ]
    )
    scaled = scale_ens * adjoint
    deep = levels * rows
    for k in range(members):
        value = jnp.sum(ensemble[k].astype(f32) * scaled, axis=0)
        field_a[k * deep : (k + 1) * deep, :] = value.reshape(deep, lanes)
    still = static_part * static_sd[...] * adjoint
    field_a[members * deep :, :] = still.reshape(variables * deep, lanes)
    sum_middle(0)

    smooth_back = smooth(PASSES)

    totals = sum_end(0)
    start_norm = totals[0:1]
    step = start_norm / (totals[1:2] + totals[2:3])
    image = direction[...] + smooth_back[...].reshape(fields, levels, rows, lanes)
    image_out[...] = image
    left = residual[...] - step * image
    next_norm = jnp.sum(left * left)
    sum_begin(1, jnp.full((8, lanes), next_norm, f32))
    sum_middle(1)
    totals = sum_end(1)
    ratio = totals / (start_norm + 1e-6)
    scalars_out[...] = jnp.where(row8 == 0, step, ratio)

    for p in range(2 * PASSES):
        for axis in AXES:
            for side in (0, 1):
                if_there(axis, side, lambda: halo_copy(p, axis, side).wait_send())
    for copy in (there, back_again):
        each(group - 1, lambda k: copy(k).wait_send())
    for turn in (0, 1):
        plane, column = sum_copies(turn)
        each(group - 1, lambda k: plane(k).wait_send())
        each(n_lev - 1, lambda k: column(k).wait_send())


def body(
    sizes,
    solution,
    residual,
    direction,
    ensemble,
    static_sd,
    send_tile,
    pair_count,
    obs_weight,
    obs_precision,
):
    n_lon, n_lat, n_lev = sizes
    members, variables, levels, rows, lanes = ensemble.shape
    fields = direction.shape[0]
    blocks = fields * levels
    group = n_lon * n_lat
    slots = send_tile.shape[4]
    height = slots * variables
    passes = 2 * PASSES
    lat_rows = -(-blocks // 16) * 16
    vmem = pl.BlockSpec(memory_space=pltpu.VMEM)
    smem = pl.BlockSpec(memory_space=pltpu.SMEM)
    dma = pltpu.SemaphoreType.DMA
    image, scalars = pl.pallas_call(
        functools.partial(kernel, sizes),
        out_shape=[
            jax.ShapeDtypeStruct(direction.shape, f32),
            jax.ShapeDtypeStruct((8, lanes), f32),
        ],
        in_specs=[vmem] * 6 + [smem] * 2,
        out_specs=[vmem] * 2,
        scratch_shapes=[
            pltpu.VMEM((blocks * rows, lanes), f32),
            pltpu.VMEM((blocks * rows, lanes), f32),
            pltpu.VMEM((passes, 2, fields * rows, lanes), bf16),
            pltpu.VMEM((passes, 2, fields * rows, lanes), bf16),
            pltpu.VMEM((passes, 2, lat_rows, lanes), bf16),
            pltpu.VMEM((passes, 2, lat_rows, lanes), bf16),
            pltpu.VMEM((passes, 2, 1, blocks * rows), f32),
            pltpu.VMEM((passes, 2, 1, blocks * rows), f32),
            pltpu.VMEM((group * height, lanes), f32),
            pltpu.VMEM((group * height, lanes), f32),
            pltpu.VMEM((group * height, lanes), f32),
            pltpu.VMEM((group * height, lanes), f32),
            pltpu.VMEM((2, 2, 8, lanes), f32),
            pltpu.VMEM((2, group, 8, lanes), f32),
            pltpu.VMEM((2, n_lev, 8, lanes), f32),
            dma((passes, 3, 2)),
            dma((passes, 3, 2)),
            dma((2, group)),
            dma((2, group)),
            dma((2, group)),
            dma((2, group)),
            dma((2, n_lev)),
            dma((2, n_lev)),
        ],
        compiler_params=pltpu.CompilerParams(
            collective_id=0, has_side_effects=True, vmem_limit_bytes=40 * 1024 * 1024
        ),
        cost_estimate=pl.CostEstimate(flops=10**8, bytes_accessed=3 * 10**6, transcendentals=0),
        name="cg_step",
    )(
        direction,
        residual,
        ensemble,
        static_sd,
        obs_weight,
        obs_precision,
        send_tile,
        pair_count,
    )
    step = scalars[0, 0]
    ratio = scalars[1, 0]
    new_residual = residual - step * image
    return (
        solution + step * direction,
        new_residual,
        new_residual + ratio * direction,
    )


def solution(mesh):
    sizes = tuple(mesh.shape[axis] for axis in AXES)
    field = P(None, "lev", "lat", "lon")
    in_specs = (
        field,
        field,
        field,
        P(None, None, "lev", "lat", "lon"),
        field,
        P("lev", "lon", "lat", None, None),
        P("lev", "lon", "lat", None),
        P("lev", "lon", "lat", None, None, None, None),
        P("lev", "lon", "lat", None, None, None),
    )
    return jax.shard_map(
        functools.partial(body, sizes),
        mesh=mesh,
        in_specs=in_specs,
        out_specs=(field, field, field),
        check_vma=False,
    )
```

time: 327 us -> 58.9 us (0.18)
  waiting for transfers between devices: 161 us -> 0 us
  blocking collectives: 80.7 us -> 0 us
  Pallas kernels: 0 us -> 49 us
  starting transfers between devices: 39.8 us -> 0 us
  other arithmetic: 31.2 us -> 2.22 us
  local copies, waits for them, and re-layouts: 9.95 us -> 6.67 us
    ppermute x24 -> x0, waiting for transfers between devices: 148 us -> none  [the longest x12 121 us: with_halo(): lax.ppermute(lax.slice_in_dim(block, block.shape[dim] - width, None, axis...]
    psum x2 -> x0, blocking collectives: 80.7 us -> none  [the longest x1 40.5 us: body(): lax.psum(jnp.sum(new_residual * new_residual), ('lon', 'lat', 'lev'))]
    pallas_call x0 -> x1, Pallas kernels: none -> 49 us  [body(): pl.pallas_call(functools.partial(kernel, sizes), out_shape=[jax.ShapeDtyp...]
    ppermute x24 -> x0, starting transfers between devices: 32.1 us -> none  [the longest x12 22 us: with_halo(): lax.ppermute(lax.slice_in_dim(block, 0, width, axis=dim), axis, backward)]
    mul x10 -> x0, other arithmetic: 20.3 us -> none  [the longest x9 20.3 us: smooth(): fields = one_pass(padded * inside) * inside[1:-1, 1:-1]]
    all_to_all x2 -> x0, waiting for transfers between devices: 13.2 us -> none  [the longest x1 6.65 us: body(): lax.all_to_all(returned, ('lon', 'lat'), split_axis=0, concat_axis=0, til...]
    all_to_all x2 -> x0, starting transfers between devices: 7.62 us -> none  [the longest x1 4.28 us: body(): lax.all_to_all(outgoing, ('lon', 'lat'), split_axis=0, concat_axis=0, til...]
  transfers between devices with their start and end apart: 26 -> 0, of which waited for: 26 -> 0; matrix products, arithmetic and copies ran while one was open for 1% -> 0% of each run, Pallas kernels for 0% -> 0%
where the time goes in v1:
time: 58.9 us; the launch traced here: 58.5 us
  Pallas kernels  49 us (83%)
  local copies, waits for them, and re-layouts  6.67 us (11%)
  other arithmetic  2.22 us (4%)
  between operations  0.66 us (1%)
    pallas_call x1, Pallas kernels, body(): pl.pallas_call(functools.partial(kernel, sizes), out_shape=[jax.ShapeDtyp...  49 us
    unnamed x17, local copies, waits for them, and re-layouts  6.09 us
    add x1, other arithmetic, body(): new_residual + ratio * direction  2.22 us

profile of v1, /device:TPU:0, one launch (start us, length us, event | category | flops | bytes accessed | tf_op | source)
XLA Modules:
  0.0 58.5 jit_solution(11970653381443915618)
XLA Ops:
  0.6 0.0 copy-start.6
  0.6 0.8 %copy.12.send_tile = s32[1,1,1,8,2]{4,3,2,1,0:T(8,128)S(1)} copy(s32[1,1,1,8,2]{3,4,2,1,0:T(2,128)} %param.14) | data formatting | bytes 128 | tf_op args[5]
  1.4 0.0 copy-done.6
  1.4 0.0 copy-start
  1.4 1.0 %copy-done = f32[36,2,8,128]{3,2,1,0:T(8,128)S(1)} copy-done((f32[36,2,8,128]{3,2,1,0:T(8,128)S(1)}, f32[36,2,8,128]{3,2,1,0:T(8,128)}, u32[]{:S(2)}) %copy-start) | copy-done | bytes 294936
  2.4 0.0 copy-start.1
  2.4 1.0 %copy-done.1 = f32[36,2,8,128]{3,2,1,0:T(8,128)S(1)} copy-done((f32[36,2,8,128]{3,2,1,0:T(8,128)S(1)}, f32[36,2,8,128]{3,2,1,0:T(8,128)}, u32[]{:S(2)}) %copy-start.1) | copy-done | bytes 294936
  3.3 0.0 copy-start.2
  3.3 1.0 %copy-done.2 = bf16[32,4,2,8,128]{4,3,2,1,0:T(8,128)(2,1)S(1)} copy-done((bf16[32,4,2,8,128]{4,3,2,1,0:T(8,128)(2,1)S(1)}, bf16[32,4,2,8,128]{4,3,2,1,0:T(8,128)(2,1)}, u32[]{:S(2)}) %copy-start.2) | copy-done | bytes 524312
  4.4 0.0 copy-start.3
  4.4 0.9 %copy-done.3 = bf16[1,1,1,8,2,8,512]{6,5,4,3,2,1,0:T(8,128)(2,1)S(1)} copy-done((bf16[1,1,1,8,2,8,512]{6,5,4,3,2,1,0:T(8,128)(2,1)S(1)}, bf16[1,1,1,8,2,8,512]{6,5,4,3,2,1,0:T(8,128)(2,1)}, u32[]{:S(2)}) %copy-start.3) | copy-done | bytes 131096
  5.3 0.0 copy-start.4
  5.3 0.8 %copy-done.4 = f32[4,2,8,128]{3,2,1,0:T(8,128)S(1)} copy-done((f32[4,2,8,128]{3,2,1,0:T(8,128)S(1)}, f32[4,2,8,128]{3,2,1,0:T(8,128)}, u32[]{:S(2)}) %copy-start.4) | copy-done | bytes 32792
  6.0 0.0 copy-start.5
  6.0 0.7 %copy-done.5 = f32[1,1,1,8,2,8]{5,4,3,2,1,0:T(2,128)S(1)} copy-done((f32[1,1,1,8,2,8]{5,4,3,2,1,0:T(2,128)S(1)}, f32[1,1,1,8,2,8]{5,4,3,2,1,0:T(2,128)}, u32[]{:S(2)}) %copy-start.5) | copy-done | bytes 536
  6.7 0.0 copy-start.7
  6.7 49.0 %cg_step.1 = (f32[36,2,8,128]{3,2,1,0:T(8,128)S(1)}, f32[8,128]{1,0:T(8,128)S(1)}) custom-call(f32[36,2,8,128]{3,2,1,0:T(8,128)S(1)} %copy-done, f32[36,2,8,128]{3,2,1,0:T(8,128)S(1)} %copy-done.1, bf16[32,4,2,8,128]{4,3,2,1,0:T(8,128)(2,1)S(1)} %copy-done.2, f32[4,2,8,128]{3,2,1,0:T(8,128)S(1)} %copy-done.4, ...), custom_call_target="tpu_custom_call" | custom-call | flops 100000000 | bytes 3000000 | tf_op jit(solution)/shard_map/cg_step/pallas_call | solution.py:443
  55.7 0.6 fusion
  56.3 0.0 copy-done.7
  56.3 2.2 %multiply_add_fusion = (f32[36,2,8,128]{3,2,1,0:T(8,128)}, f32[36,2,8,128]{3,2,1,0:T(8,128)}, f32[36,2,8,128]{3,2,1,0:T(8,128)}) fusion(f32[36,2,8,128]{3,2,1,0:T(8,128)S(1)} %copy-done, f32[]{:T(128)} %bitcast.1, f32[36,2,8,128]{3,2,1,0:T(8,128)S(1)} %copy-done.1, f32[36,2,8,128]{3,2,1,0:T(8,128)S(1)} %get-tuple-element.6, f32[]{:T(128)} %bitcast, ...), kind=kLoop, calls=%fused_computation | loop fusion | flops 442368 | bytes 2064392 | tf_op jit(solution)/shard_map/add | solution.py:497
Async XLA Ops:
  0.6 0.8 %copy-start.6 = (s32[1,1,1,8]{3,2,1,0:T(1,128)S(1)}, s32[1,1,1,8]{3,2,1,0:T(1,128)}, u32[]{:S(2)}) copy-start(s32[1,1,1,8]{3,2,1,0:T(1,128)} %pair_count.1) | copy-start | bytes 100
  1.4 1.0 %copy-start = (f32[36,2,8,128]{3,2,1,0:T(8,128)S(1)}, f32[36,2,8,128]{3,2,1,0:T(8,128)}, u32[]{:S(2)}) copy-start(f32[36,2,8,128]{3,2,1,0:T(8,128)} %direction.1) | copy-start | bytes 884740
  2.4 1.0 %copy-start.1 = (f32[36,2,8,128]{3,2,1,0:T(8,128)S(1)}, f32[36,2,8,128]{3,2,1,0:T(8,128)}, u32[]{:S(2)}) copy-start(f32[36,2,8,128]{3,2,1,0:T(8,128)} %residual.1) | copy-start | bytes 884740
  3.3 1.0 %copy-start.2 = (bf16[32,4,2,8,128]{4,3,2,1,0:T(8,128)(2,1)S(1)}, bf16[32,4,2,8,128]{4,3,2,1,0:T(8,128)(2,1)}, u32[]{:S(2)}) copy-start(bf16[32,4,2,8,128]{4,3,2,1,0:T(8,128)(2,1)} %ensemble.1) | copy-start | bytes 1572868
  4.4 0.9 %copy-start.3 = (bf16[1,1,1,8,2,8,512]{6,5,4,3,2,1,0:T(8,128)(2,1)S(1)}, bf16[1,1,1,8,2,8,512]{6,5,4,3,2,1,0:T(8,128)(2,1)}, u32[]{:S(2)}) copy-start(bf16[1,1,1,8,2,8,512]{6,5,4,3,2,1,0:T(8,128)(2,1)} %obs_weight.1) | copy-start | bytes 393220
  5.3 0.8 %copy-start.4 = (f32[4,2,8,128]{3,2,1,0:T(8,128)S(1)}, f32[4,2,8,128]{3,2,1,0:T(8,128)}, u32[]{:S(2)}) copy-start(f32[4,2,8,128]{3,2,1,0:T(8,128)} %static_sd.1) | copy-start | bytes 98308
  6.0 0.7 %copy-start.5 = (f32[1,1,1,8,2,8]{5,4,3,2,1,0:T(2,128)S(1)}, f32[1,1,1,8,2,8]{5,4,3,2,1,0:T(2,128)}, u32[]{:S(2)}) copy-start(f32[1,1,1,8,2,8]{5,4,3,2,1,0:T(2,128)} %obs_precision.1) | copy-start | bytes 1540
  6.7 49.6 %copy-start.7 = (f32[36,2,8,128]{3,2,1,0:T(8,128)S(1)}, f32[36,2,8,128]{3,2,1,0:T(8,128)}, u32[]{:S(2)}) copy-start(f32[36,2,8,128]{3,2,1,0:T(8,128)} %param.9) | copy-start | bytes 884740

commit v2 on v1

--- a/solution.py
+++ b/solution.py
@@ -14,6 +14,7 @@
 static_part = 0.5
 centre_share = 1.0 - 2.0 * (spread_lon + spread_lat + spread_lev)
 PASSES = 4
+PARTS = 2
 AXES = ("lon", "lat", "lev")
 MESH = pl.DeviceIdType.MESH
 f32 = jnp.float32
@@ -30,16 +31,24 @@
 
 def kernel(
     sizes,
+    direction_hbm,
+    residual_hbm,
+    ensemble_hbm,
+    static_sd_hbm,
+    obs_weight_hbm,
+    obs_precision_hbm,
+    send_tile,
+    pair_count,
+    image_out,
+    step_out,
+    ratio_out,
     direction,
     residual,
     ensemble,
     static_sd,
     obs_weight,
     obs_precision,
-    send_tile,
-    pair_count,
-    image_out,
-    scalars_out,
+    fetch_sem,
     field_a,
     field_b,
     lev_send,
@@ -69,10 +78,25 @@
     fields = direction.shape[0]
     blocks = fields * levels
     group = n_lon * n_lat
-    slots = send_tile.shape[4]
+    slots = send_tile.shape[3]
     tiles = levels * rows
     scale_ens = (ens_share / members) ** 0.5
     at_lon, at_lat, at_lev = (lax.axis_index(a) for a in AXES)
+    held = (direction, residual, ensemble, static_sd, obs_weight, obs_precision)
+    origins = (
+        direction_hbm,
+        residual_hbm,
+        ensemble_hbm,
+        static_sd_hbm,
+        obs_weight_hbm,
+        obs_precision_hbm,
+    )
+    fetches = [
+        pltpu.make_async_copy(src, dst, fetch_sem.at[i])
+        for i, (src, dst) in enumerate(zip(origins, held))
+    ]
+    for fetch in fetches:
+        fetch.start()
     me = at_lon * n_lat + at_lat
 
     def plane_id(k):
@@ -96,15 +120,15 @@
     buffers = {"lev": (lev_send, lev_recv), "lat": (lat_send, lat_recv), "lon": (lon_send, lon_recv)}
     places = {"lev": (at_lev, n_lev), "lat": (at_lat, n_lat), "lon": (at_lon, n_lon)}
 
-    def halo_copy(p, axis, side):
+    def halo_copy(p, h, axis, side):
         src, dst = buffers[axis]
         place, count = places[axis]
         number = AXES.index(axis)
         return pltpu.make_async_remote_copy(
-            src_ref=src.at[p, side],
-            dst_ref=dst.at[p, 1 - side],
-            send_sem=halo_ssem.at[p, number, side],
-            recv_sem=halo_rsem.at[p, number, 1 - side],
+            src_ref=src.at[p, h, side],
+            dst_ref=dst.at[p, h, 1 - side],
+            send_sem=halo_ssem.at[p, h, number, side],
+            recv_sem=halo_rsem.at[p, h, number, 1 - side],
             device_id={axis: lax.rem(place + (count - 1 if side == 0 else 1), count)},
             device_id_type=MESH,
         )
@@ -126,31 +150,36 @@
     edge_lane = lax.broadcasted_iota(jnp.int32, (8, lanes), 1)
     edges = ((edge_row == 0) & (edge_lane == 0)) | ((edge_row == 1) & (edge_lane == lanes - 1))
     edges = edges.astype(bf16)
-    lat_pad = lat_send.shape[2] - blocks
-
-    def send_halos(p, src):
-        x4 = src[...].reshape(fields, levels, rows, lanes)
+    part_fields = fields // PARTS
+    part_blocks = part_fields * levels
+    part_rows = part_blocks * rows
+    lat_pad = lat_send.shape[3] - part_blocks
+
+    def send_halos(p, h, src):
+        start = h * part_rows
+        x = src[start : start + part_rows, :]
+        x4 = x.reshape(part_fields, levels, rows, lanes)
         for side, level in ((0, 0), (1, levels - 1)):
-            lev_send[p, side] = x4[:, level].reshape(fields * rows, lanes).astype(bf16)
-            if_there("lev", side, lambda side=side: halo_copy(p, "lev", side).start())
+            lev_send[p, h, side] = x4[:, level].reshape(part_fields * rows, lanes).astype(bf16)
+            if_there("lev", side, lambda side=side: halo_copy(p, h, "lev", side).start())
+        packed = lax.dot_general(
+            edges, x.astype(bf16), (((1,), (1,)), ((), ())), preferred_element_type=f32
+        )
         for side, row in ((0, 0), (1, rows - 1)):
-            edge = src[pl.ds(row, blocks, stride=rows), :]
+            edge = src[pl.ds(start + row, part_blocks, stride=rows), :]
             if lat_pad:
                 edge = jnp.concatenate([edge, jnp.zeros((lat_pad, lanes), f32)], axis=0)
-            lat_send[p, side] = edge.astype(bf16)
-            if_there("lat", side, lambda side=side: halo_copy(p, "lat", side).start())
-        packed = lax.dot_general(
-            edges, src[...].astype(bf16), (((1,), (1,)), ((), ())), preferred_element_type=f32
-        )
+            lat_send[p, h, side] = edge.astype(bf16)
+            if_there("lat", side, lambda side=side: halo_copy(p, h, "lat", side).start())
         for side in (0, 1):
-            lon_send[p, side] = packed[side : side + 1]
-            halo_copy(p, "lon", side).start()
-
-    chunk = max(c for c in range(1, 13) if fields % c == 0)
-
-    def local_part(src, dst):
-        for first in range(0, fields, chunk):
-            span = pl.ds(first * levels * rows, chunk * levels * rows)
+            lon_send[p, h, side] = packed[side : side + 1]
+            halo_copy(p, h, "lon", side).start()
+
+    chunk = max(c for c in range(1, 10) if part_fields % c == 0)
+
+    def local_part(h, src, dst):
+        for first in range(0, part_fields, chunk):
+            span = pl.ds(h * part_rows + first * levels * rows, chunk * levels * rows)
             x = src[span, :].reshape(chunk * levels, rows, lanes)
             y = x * centre_share
             y = y + west * pltpu.roll(x, 1, 2) + east * pltpu.roll(x, lanes - 1, 2)
@@ -163,51 +192,56 @@
                 y = y + spread_lev * (above + below).reshape(chunk * levels, rows, lanes)
             dst[span, :] = y.reshape(chunk * levels * rows, lanes)
 
-    def add_halos(p, dst):
+    def add_halos(p, h, dst):
+        start = h * part_rows
         for side in (0, 1):
-            halo_copy(p, "lon", 1 - side).wait_recv()
+            halo_copy(p, h, "lon", 1 - side).wait_recv()
         ends = jnp.concatenate(
-            [lon_recv[p, 0], lon_recv[p, 1], jnp.zeros((6, blocks * rows), f32)], axis=0
+            [lon_recv[p, h, 0], lon_recv[p, h, 1], jnp.zeros((6, part_rows), f32)], axis=0
         )
         spill = lax.dot_general(
             ends.astype(bf16), edges, (((0,), (0,)), ((), ())), preferred_element_type=f32
         )
-        dst[...] += spread_lon * spill
         for side, row in ((0, 0), (1, rows - 1)):
-            if_there("lat", side, lambda side=side: halo_copy(p, "lat", 1 - side).wait_recv())
-            edge = lat_recv[p, side].astype(f32)[:blocks]
-            at = pl.ds(row, blocks, stride=rows)
+            if_there("lat", side, lambda side=side: halo_copy(p, h, "lat", 1 - side).wait_recv())
+            edge = lat_recv[p, h, side].astype(f32)[:part_blocks]
+            at = pl.ds(start + row, part_blocks, stride=rows)
             dst[at, :] = dst[at, :] + spread_lat * edge
         for side in (0, 1):
-            if_there("lev", side, lambda side=side: halo_copy(p, "lev", 1 - side).wait_recv())
-        low = lev_recv[p, 0].astype(f32).reshape(fields, 1, rows, lanes) * spread_lev
-        high = lev_recv[p, 1].astype(f32).reshape(fields, 1, rows, lanes) * spread_lev
-        y4 = dst[...].reshape(fields, levels, rows, lanes)
+            if_there("lev", side, lambda side=side: halo_copy(p, h, "lev", 1 - side).wait_recv())
+        low = lev_recv[p, h, 0].astype(f32).reshape(part_fields, 1, rows, lanes) * spread_lev
+        high = lev_recv[p, h, 1].astype(f32).reshape(part_fields, 1, rows, lanes) * spread_lev
+        y = dst[start : start + part_rows, :] + spread_lon * spill
+        y4 = y.reshape(part_fields, levels, rows, lanes)
         if levels == 1:
             y4 = y4 + low + high
         else:
             inner = [y4[:, 1:-1]] if levels > 2 else []
             y4 = jnp.concatenate([y4[:, :1] + low, *inner, y4[:, -1:] + high], axis=1)
-        dst[...] = y4.reshape(blocks * rows, lanes)
-
-    def smooth(first_pass):
+        dst[start : start + part_rows, :] = y4.reshape(part_rows, lanes)
+
+    def smooth(first_pass, meanwhile):
         src, dst = field_a, field_b
         for p in range(first_pass, first_pass + PASSES):
-            send_halos(p, src)
-            local_part(src, dst)
-            add_halos(p, dst)
+            for h in range(PARTS):
+                if p == first_pass and h == 0:
+                    meanwhile()
+                local_part(h, src, dst)
+                add_halos(p, h, dst)
+                if p < first_pass + PASSES - 1:
+                    send_halos(p + 1, h, dst)
             src, dst = dst, src
         return src
 
-    field_a[...] = direction[...].reshape(blocks * rows, lanes)
     for side in (0, 1):
         for axis in ("lat", "lev"):
             place, count = places[axis]
 
             def clear(axis=axis, side=side):
+                ref = buffers[axis][1]
                 for p in range(2 * PASSES):
-                    ref = buffers[axis][1]
-                    ref[p, side] = jnp.zeros(ref.shape[2:], ref.dtype)
+                    for h in range(PARTS):
+                        ref[p, h, side] = jnp.zeros(ref.shape[3:], ref.dtype)
 
             pl.when(place == 0 if side == 0 else place == count - 1)(clear)
 
@@ -215,7 +249,7 @@
 
     def slot_code(i):
         s, d = i // group, i % group
-        tile = send_tile[0, 0, 0, d, s]
+        tile = send_tile[0, 0, 0, s, d]
         return jnp.where(s < pair_count[0, 0, 0, d], tile, -1)
 
     def fill(dim, shape):
@@ -237,18 +271,27 @@
         lax.broadcasted_iota(jnp.int32, (1, obs, obs), 1)
         == lax.broadcasted_iota(jnp.int32, (1, obs, obs), 2)
     ).astype(f32)
-    precision = [
-        jnp.sum(obs_precision[0, 0, 0][:, s : s + 1, :] * eye, axis=2, keepdims=True)
-        for s in range(slots)
-    ]
-    d_all = direction[...]
-    r_all = residual[...]
-    direction_norm = jnp.sum(d_all * d_all)
-    residual_norm = jnp.sum(r_all * r_all)
-
+    fetches[0].wait()
+    field_a[...] = direction[...].reshape(blocks * rows, lanes)
     pl.semaphore_wait(barrier, group - 1 + n_lev - 1)
-
-    smoothed = smooth(0)
+    for h in range(PARTS):
+        send_halos(0, h, field_a)
+
+    known = []
+
+    def local_sums():
+        for fetch in fetches[1:]:
+            fetch.wait()
+        for s in range(slots):
+            row = obs_precision[0, 0, 0][:, s : s + 1, :]
+            known.append(jnp.sum(row * eye, axis=2, keepdims=True))
+        d_all = direction[...]
+        r_all = residual[...]
+        known.append(jnp.sum(d_all * d_all))
+        known.append(jnp.sum(r_all * r_all))
+
+    smoothed = smooth(0, local_sums)
+    precision, direction_norm, residual_norm = known[:slots], known[slots], known[slots + 1]
 
     sm4 = smoothed[...].reshape(fields, levels, rows, lanes)
     ens_part = jnp.zeros((variables, levels, rows, lanes), f32)
@@ -382,14 +425,19 @@
     )
     scaled = scale_ens * adjoint
     deep = levels * rows
+    def tell(k):
+        if (k + 1) % part_fields == 0:
+            send_halos(PASSES, (k + 1) // part_fields - 1, field_a)
+
     for k in range(members):
         value = jnp.sum(ensemble[k].astype(f32) * scaled, axis=0)
         field_a[k * deep : (k + 1) * deep, :] = value.reshape(deep, lanes)
+        tell(k)
     still = static_part * static_sd[...] * adjoint
     field_a[members * deep :, :] = still.reshape(variables * deep, lanes)
-    sum_middle(0)
-
-    smooth_back = smooth(PASSES)
+    send_halos(PASSES, PARTS - 1, field_a)
+
+    smooth_back = smooth(PASSES, lambda: sum_middle(0))
 
     totals = sum_end(0)
     start_norm = totals[0:1]
@@ -402,12 +450,14 @@
     sum_middle(1)
     totals = sum_end(1)
     ratio = totals / (start_norm + 1e-6)
-    scalars_out[...] = jnp.where(row8 == 0, step, ratio)
+    step_out[...] = jnp.broadcast_to(step, (8, lanes))
+    ratio_out[...] = ratio
 
     for p in range(2 * PASSES):
-        for axis in AXES:
-            for side in (0, 1):
-                if_there(axis, side, lambda: halo_copy(p, axis, side).wait_send())
+        for h in range(PARTS):
+            for axis in AXES:
+                for side in (0, 1):
+                    if_there(axis, side, lambda: halo_copy(p, h, axis, side).wait_send())
     for copy in (there, back_again):
         each(group - 1, lambda k: copy(k).wait_send())
     for turn in (0, 1):
@@ -436,27 +486,36 @@
     slots = send_tile.shape[4]
     height = slots * variables
     passes = 2 * PASSES
-    lat_rows = -(-blocks // 16) * 16
+    part = fields // PARTS
+    lat_rows = -(-(part * levels) // 16) * 16
     vmem = pl.BlockSpec(memory_space=pltpu.VMEM)
     smem = pl.BlockSpec(memory_space=pltpu.SMEM)
     dma = pltpu.SemaphoreType.DMA
-    image, scalars = pl.pallas_call(
+    image, step, ratio = pl.pallas_call(
         functools.partial(kernel, sizes),
         out_shape=[
             jax.ShapeDtypeStruct(direction.shape, f32),
             jax.ShapeDtypeStruct((8, lanes), f32),
+            jax.ShapeDtypeStruct((8, lanes), f32),
         ],
-        in_specs=[vmem] * 6 + [smem] * 2,
-        out_specs=[vmem] * 2,
+        in_specs=[pl.BlockSpec(memory_space=pl.ANY)] * 6 + [smem] * 2,
+        out_specs=[vmem] * 3,
         scratch_shapes=[
+            pltpu.VMEM(direction.shape, f32),
+            pltpu.VMEM(residual.shape, f32),
+            pltpu.VMEM(ensemble.shape, bf16),
+            pltpu.VMEM(static_sd.shape, f32),
+            pltpu.VMEM(obs_weight.shape, bf16),
+            pltpu.VMEM(obs_precision.shape, f32),
+            dma((6,)),
             pltpu.VMEM((blocks * rows, lanes), f32),
             pltpu.VMEM((blocks * rows, lanes), f32),
-            pltpu.VMEM((passes, 2, fields * rows, lanes), bf16),
-            pltpu.VMEM((passes, 2, fields * rows, lanes), bf16),
-            pltpu.VMEM((passes, 2, lat_rows, lanes), bf16),
-            pltpu.VMEM((passes, 2, lat_rows, lanes), bf16),
-            pltpu.VMEM((passes, 2, 1, blocks * rows), f32),
-            pltpu.VMEM((passes, 2, 1, blocks * rows), f32),
+            pltpu.VMEM((passes, PARTS, 2, part * rows, lanes), bf16),
+            pltpu.VMEM((passes, PARTS, 2, part * rows, lanes), bf16),
+            pltpu.VMEM((passes, PARTS, 2, lat_rows, lanes), bf16),
+            pltpu.VMEM((passes, PARTS, 2, lat_rows, lanes), bf16),
+            pltpu.VMEM((passes, PARTS, 2, 1, part * levels * rows), f32),
+            pltpu.VMEM((passes, PARTS, 2, 1, part * levels * rows), f32),
             pltpu.VMEM((group * height, lanes), f32),
             pltpu.VMEM((group * height, lanes), f32),
             pltpu.VMEM((group * height, lanes), f32),
@@ -464,8 +523,8 @@
             pltpu.VMEM((2, 2, 8, lanes), f32),
             pltpu.VMEM((2, group, 8, lanes), f32),
             pltpu.VMEM((2, n_lev, 8, lanes), f32),
-            dma((passes, 3, 2)),
-            dma((passes, 3, 2)),
+            dma((passes, PARTS, 3, 2)),
+            dma((passes, PARTS, 3, 2)),
             dma((2, group)),
             dma((2, group)),
             dma((2, group)),
@@ -474,7 +533,7 @@
             dma((2, n_lev)),
         ],
         compiler_params=pltpu.CompilerParams(
-            collective_id=0, has_side_effects=True, vmem_limit_bytes=40 * 1024 * 1024
+            collective_id=0, has_side_effects=True, vmem_limit_bytes=56 * 1024 * 1024
         ),
         cost_estimate=pl.CostEstimate(flops=10**8, bytes_accessed=3 * 10**6, transcendentals=0),
         name="cg_step",
@@ -485,11 +544,9 @@
         static_sd,
         obs_weight,
         obs_precision,
-        send_tile,
+        jnp.swapaxes(send_tile, 3, 4),
         pair_count,
     )
-    step = scalars[0, 0]
-    ratio = scalars[1, 0]
     new_residual = residual - step * image
     return (
         solution + step * direction,

time: 58.9 us -> 54.5 us (0.925)
  local copies, waits for them, and re-layouts: 6.67 us -> 0.65 us
  Pallas kernels: 49 us -> 50.9 us
    unnamed x17 -> x8, local copies, waits for them, and re-layouts: 6.09 us -> 0.65 us
    pallas_call x1, Pallas kernels: 49 us -> 50.9 us  [body(): pl.pallas_call(functools.partial(kernel, sizes), out_shape=[jax.ShapeDtyp...]
where the time goes in v2:
time: 54.5 us; the launch traced here: 54.2 us
  Pallas kernels  50.9 us (93%)
  other arithmetic  1.93 us (4%)
  between operations  0.7 us (1%)
  local copies, waits for them, and re-layouts  0.65 us (1%)
    pallas_call x1, Pallas kernels, body(): pl.pallas_call(functools.partial(kernel, sizes), out_shape=[jax.ShapeDtyp...  50.9 us
    add x1, other arithmetic, body(): new_residual + ratio * direction  1.93 us

profile of v2, /device:TPU:0, one launch (start us, length us, event | category | flops | bytes accessed | tf_op | source)
XLA Modules:
  0.0 54.2 jit_solution(8905702335904581913)
XLA Ops:
  0.6 0.0 copy-start
  0.6 0.0 copy-start.1
  0.7 0.0 copy-start.2
  0.7 50.9 %cg_step.1 = (f32[36,2,8,128]{3,2,1,0:T(8,128)}, f32[8,128]{1,0:T(8,128)}, f32[8,128]{1,0:T(8,128)}) custom-call(f32[36,2,8,128]{3,2,1,0:T(8,128)} %direction_hbm.1, f32[36,2,8,128]{3,2,1,0:T(8,128)} %residual_hbm.1, bf16[32,4,2,8,128]{4,3,2,1,0:T(8,128)(2,1)} %ensemble_hbm.1, f32[4,2,8,128]{3,2,1,0:T(8,128)} %static_sd_hbm.1, ...), custom_call_target="tpu_custom_call" | custom-call | flops 100000000 | bytes 3000000 | tf_op jit(solution)/shard_map/cg_step/pallas_call | solution.py:494
  51.6 0.0 copy-start.3
  51.6 0.0 copy-done
  51.6 0.0 copy-done.1
  51.6 0.0 copy-done.2
  51.6 0.6 %copy-done.3 = f32[8,128]{1,0:T(8,128)S(1)} copy-done((f32[8,128]{1,0:T(8,128)S(1)}, f32[8,128]{1,0:T(8,128)}, u32[]{:S(2)}) %copy-start.3) | copy-done | bytes 4120
  52.3 1.9 %multiply_add_fusion = (f32[36,2,8,128]{3,2,1,0:T(8,128)}, f32[36,2,8,128]{3,2,1,0:T(8,128)}, f32[36,2,8,128]{3,2,1,0:T(8,128)}) fusion(f32[36,2,8,128]{3,2,1,0:T(8,128)S(1)} %copy-done, f32[8,128]{1,0:T(8,128)} %get-tuple-element.8, f32[36,2,8,128]{3,2,1,0:T(8,128)S(1)} %copy-done.1, f32[36,2,8,128]{3,2,1,0:T(8,128)} %get-tuple-element.7, ...), kind=kLoop, calls=%fused_computation | loop fusion | flops 442368 | bytes 2072576 | tf_op jit(solution)/shard_map/add | solution.py:554
Async XLA Ops:
  0.6 51.0 %copy-start = (f32[36,2,8,128]{3,2,1,0:T(8,128)S(1)}, f32[36,2,8,128]{3,2,1,0:T(8,128)}, u32[]{:S(2)}) copy-start(f32[36,2,8,128]{3,2,1,0:T(8,128)} %direction_hbm.1) | copy-start | bytes 884740
  0.6 51.0 %copy-start.1 = (f32[36,2,8,128]{3,2,1,0:T(8,128)S(1)}, f32[36,2,8,128]{3,2,1,0:T(8,128)}, u32[]{:S(2)}) copy-start(f32[36,2,8,128]{3,2,1,0:T(8,128)} %residual_hbm.1) | copy-start | bytes 884740
  0.7 51.0 %copy-start.2 = (f32[36,2,8,128]{3,2,1,0:T(8,128)S(1)}, f32[36,2,8,128]{3,2,1,0:T(8,128)}, u32[]{:S(2)}) copy-start(f32[36,2,8,128]{3,2,1,0:T(8,128)} %param.9) | copy-start | bytes 884740
  51.6 0.7 %copy-start.3 = (f32[8,128]{1,0:T(8,128)S(1)}, f32[8,128]{1,0:T(8,128)}, u32[]{:S(2)}) copy-start(f32[8,128]{1,0:T(8,128)} %get-tuple-element.6) | copy-start | bytes 12292

commit v3 on v2

--- a/solution.py
+++ b/solution.py
@@ -120,16 +120,20 @@
     buffers = {"lev": (lev_send, lev_recv), "lat": (lat_send, lat_recv), "lon": (lon_send, lon_recv)}
     places = {"lev": (at_lev, n_lev), "lat": (at_lat, n_lat), "lon": (at_lon, n_lon)}
 
+    beside = {
+        axis: [lax.rem(place + count - 1, count), lax.rem(place + 1, count)]
+        for axis, (place, count) in places.items()
+    }
+
     def halo_copy(p, h, axis, side):
         src, dst = buffers[axis]
-        place, count = places[axis]
         number = AXES.index(axis)
         return pltpu.make_async_remote_copy(
             src_ref=src.at[p, h, side],
             dst_ref=dst.at[p, h, 1 - side],
             send_sem=halo_ssem.at[p, h, number, side],
             recv_sem=halo_rsem.at[p, h, number, 1 - side],
-            device_id={axis: lax.rem(place + (count - 1 if side == 0 else 1), count)},
+            device_id={axis: beside[axis][side]},
             device_id_type=MESH,
         )
 
@@ -158,21 +162,24 @@
     def send_halos(p, h, src):
         start = h * part_rows
         x = src[start : start + part_rows, :]
+        packed = lax.dot_general(
+            edges, x.astype(bf16), (((1,), (1,)), ((), ())), preferred_element_type=f32
+        )
         x4 = x.reshape(part_fields, levels, rows, lanes)
         for side, level in ((0, 0), (1, levels - 1)):
             lev_send[p, h, side] = x4[:, level].reshape(part_fields * rows, lanes).astype(bf16)
-            if_there("lev", side, lambda side=side: halo_copy(p, h, "lev", side).start())
-        packed = lax.dot_general(
-            edges, x.astype(bf16), (((1,), (1,)), ((), ())), preferred_element_type=f32
-        )
         for side, row in ((0, 0), (1, rows - 1)):
             edge = src[pl.ds(start + row, part_blocks, stride=rows), :]
             if lat_pad:
                 edge = jnp.concatenate([edge, jnp.zeros((lat_pad, lanes), f32)], axis=0)
             lat_send[p, h, side] = edge.astype(bf16)
-            if_there("lat", side, lambda side=side: halo_copy(p, h, "lat", side).start())
         for side in (0, 1):
             lon_send[p, h, side] = packed[side : side + 1]
+        for side in (0, 1):
+            if_there("lev", side, lambda: halo_copy(p, h, "lev", side).start())
+        for side in (0, 1):
+            if_there("lat", side, lambda: halo_copy(p, h, "lat", side).start())
+        for side in (0, 1):
             halo_copy(p, h, "lon", side).start()
 
     chunk = max(c for c in range(1, 10) if part_fields % c == 0)
@@ -194,8 +201,9 @@
 
     def add_halos(p, h, dst):
         start = h * part_rows
-        for side in (0, 1):
-            halo_copy(p, h, "lon", 1 - side).wait_recv()
+        for axis in AXES:
+            for side in (0, 1):
+                if_there(axis, side, lambda: halo_copy(p, h, axis, 1 - side).wait_recv())
         ends = jnp.concatenate(
             [lon_recv[p, h, 0], lon_recv[p, h, 1], jnp.zeros((6, part_rows), f32)], axis=0
         )
@@ -203,12 +211,9 @@
             ends.astype(bf16), edges, (((0,), (0,)), ((), ())), preferred_element_type=f32
         )
         for side, row in ((0, 0), (1, rows - 1)):
-            if_there("lat", side, lambda side=side: halo_copy(p, h, "lat", 1 - side).wait_recv())
             edge = lat_recv[p, h, side].astype(f32)[:part_blocks]
             at = pl.ds(start + row, part_blocks, stride=rows)
             dst[at, :] = dst[at, :] + spread_lat * edge
-        for side in (0, 1):
-            if_there("lev", side, lambda side=side: halo_copy(p, h, "lev", 1 - side).wait_recv())
         low = lev_recv[p, h, 0].astype(f32).reshape(part_fields, 1, rows, lanes) * spread_lev
         high = lev_recv[p, h, 1].astype(f32).reshape(part_fields, 1, rows, lanes) * spread_lev
         y = dst[start : start + part_rows, :] + spread_lon * spill

time: 54.5 us -> 55.1 us (1.011)
  Pallas kernels: 50.9 us -> 51.5 us
    pallas_call x1, Pallas kernels: 50.9 us -> 51.5 us  [body(): pl.pallas_call(functools.partial(kernel, sizes), out_shape=[jax.ShapeDtyp...]
where the time goes in v3:
time: 55.1 us; the launch traced here: 54.8 us
  Pallas kernels  51.5 us (93%)
  other arithmetic  1.93 us (4%)
  between operations  0.7 us (1%)
  local copies, waits for them, and re-layouts  0.65 us (1%)
    pallas_call x1, Pallas kernels, body(): pl.pallas_call(functools.partial(kernel, sizes), out_shape=[jax.ShapeDtyp...  51.5 us
    add x1, other arithmetic, body(): new_residual + ratio * direction  1.93 us

profile of v3, /device:TPU:0, one launch (start us, length us, event | category | flops | bytes accessed | tf_op | source)
XLA Modules:
  0.0 54.8 jit_solution(14274013190264677971)
XLA Ops:
  0.6 0.0 copy-start
  0.6 0.0 copy-start.1
  0.7 0.0 copy-start.2
  0.7 51.5 %cg_step.1 = (f32[36,2,8,128]{3,2,1,0:T(8,128)}, f32[8,128]{1,0:T(8,128)}, f32[8,128]{1,0:T(8,128)}) custom-call(f32[36,2,8,128]{3,2,1,0:T(8,128)} %direction_hbm.1, f32[36,2,8,128]{3,2,1,0:T(8,128)} %residual_hbm.1, bf16[32,4,2,8,128]{4,3,2,1,0:T(8,128)(2,1)} %ensemble_hbm.1, f32[4,2,8,128]{3,2,1,0:T(8,128)} %static_sd_hbm.1, ...), custom_call_target="tpu_custom_call" | custom-call | flops 100000000 | bytes 3000000 | tf_op jit(solution)/shard_map/cg_step/pallas_call | solution.py:499
  52.2 0.0 copy-start.3
  52.2 0.0 copy-done
  52.2 0.0 copy-done.1
  52.2 0.0 copy-done.2
  52.2 0.6 %copy-done.3 = f32[8,128]{1,0:T(8,128)S(1)} copy-done((f32[8,128]{1,0:T(8,128)S(1)}, f32[8,128]{1,0:T(8,128)}, u32[]{:S(2)}) %copy-start.3) | copy-done | bytes 4120
  52.9 1.9 %multiply_add_fusion = (f32[36,2,8,128]{3,2,1,0:T(8,128)}, f32[36,2,8,128]{3,2,1,0:T(8,128)}, f32[36,2,8,128]{3,2,1,0:T(8,128)}) fusion(f32[36,2,8,128]{3,2,1,0:T(8,128)S(1)} %copy-done, f32[8,128]{1,0:T(8,128)} %get-tuple-element.8, f32[36,2,8,128]{3,2,1,0:T(8,128)S(1)} %copy-done.1, f32[36,2,8,128]{3,2,1,0:T(8,128)} %get-tuple-element.7, ...), kind=kLoop, calls=%fused_computation | loop fusion | flops 442368 | bytes 2072576 | tf_op jit(solution)/shard_map/add | solution.py:559
Async XLA Ops:
  0.6 51.6 %copy-start = (f32[36,2,8,128]{3,2,1,0:T(8,128)S(1)}, f32[36,2,8,128]{3,2,1,0:T(8,128)}, u32[]{:S(2)}) copy-start(f32[36,2,8,128]{3,2,1,0:T(8,128)} %direction_hbm.1) | copy-start | bytes 884740
  0.6 51.6 %copy-start.1 = (f32[36,2,8,128]{3,2,1,0:T(8,128)S(1)}, f32[36,2,8,128]{3,2,1,0:T(8,128)}, u32[]{:S(2)}) copy-start(f32[36,2,8,128]{3,2,1,0:T(8,128)} %residual_hbm.1) | copy-start | bytes 884740
  0.7 51.6 %copy-start.2 = (f32[36,2,8,128]{3,2,1,0:T(8,128)S(1)}, f32[36,2,8,128]{3,2,1,0:T(8,128)}, u32[]{:S(2)}) copy-start(f32[36,2,8,128]{3,2,1,0:T(8,128)} %param.9) | copy-start | bytes 884740
  52.2 0.7 %copy-start.3 = (f32[8,128]{1,0:T(8,128)S(1)}, f32[8,128]{1,0:T(8,128)}, u32[]{:S(2)}) copy-start(f32[8,128]{1,0:T(8,128)} %get-tuple-element.6) | copy-start | bytes 12292

commit v4 on v2

--- a/solution.py
+++ b/solution.py
@@ -64,6 +64,9 @@
     sum_send,
     sum_plane,
     sum_lev,
+    sum_all,
+    all_ssem,
+    all_rsem,
     halo_ssem,
     halo_rsem,
     a2a_ssem,
@@ -114,8 +117,18 @@
     def greet_lev(k):
         pl.semaphore_signal(barrier, inc=1, device_id=lev_id(k + 1), device_id_type=MESH)
 
-    each(group - 1, greet_plane)
-    each(n_lev - 1, greet_lev)
+    everyone = n_lev * group
+    flat = everyone <= 32
+
+    def any_id(q):
+        return {**plane_id(q % group)[1], **lev_id(q // group)}
+
+    if flat:
+        for q in range(1, everyone):
+            pl.semaphore_signal(barrier, inc=1, device_id=any_id(q), device_id_type=MESH)
+    else:
+        each(group - 1, greet_plane)
+        each(n_lev - 1, greet_lev)
 
     buffers = {"lev": (lev_send, lev_recv), "lat": (lat_send, lat_recv), "lon": (lon_send, lon_recv)}
     places = {"lev": (at_lev, n_lev), "lat": (at_lat, n_lat), "lon": (at_lon, n_lon)}
@@ -273,7 +286,7 @@
     ).astype(f32)
     fetches[0].wait()
     field_a[...] = direction[...].reshape(blocks * rows, lanes)
-    pl.semaphore_wait(barrier, group - 1 + n_lev - 1)
+    pl.semaphore_wait(barrier, everyone - 1 if flat else group - 1 + n_lev - 1)
     for h in range(PARTS):
         send_halos(0, h, field_a)
 
@@ -446,9 +459,31 @@
     image_out[...] = image
     left = residual[...] - step * image
     next_norm = jnp.sum(left * left)
-    sum_begin(1, jnp.full((8, lanes), next_norm, f32))
-    sum_middle(1)
-    totals = sum_end(1)
+    spread = jnp.full((8, lanes), next_norm, f32)
+
+    def to_any(q):
+        return pltpu.make_async_remote_copy(
+            src_ref=sum_all.at[0],
+            dst_ref=sum_all.at[q],
+            send_sem=all_ssem.at[q],
+            recv_sem=all_rsem.at[q],
+            device_id=any_id(q),
+            device_id_type=MESH,
+        )
+
+    if flat:
+        sum_all[0] = spread
+        for q in range(1, everyone):
+            to_any(q).start()
+        for q in range(1, everyone):
+            to_any(q).wait_recv()
+        totals = jnp.sum(sum_all[...], axis=0)
+        for q in range(1, everyone):
+            to_any(q).wait_send()
+    else:
+        sum_begin(1, spread)
+        sum_middle(1)
+        totals = sum_end(1)
     ratio = totals / (start_norm + 1e-6)
     step_out[...] = jnp.broadcast_to(step, (8, lanes))
     ratio_out[...] = ratio
@@ -460,7 +495,7 @@
                     if_there(axis, side, lambda: halo_copy(p, h, axis, side).wait_send())
     for copy in (there, back_again):
         each(group - 1, lambda k: copy(k).wait_send())
-    for turn in (0, 1):
+    for turn in (0,) if flat else (0, 1):
         plane, column = sum_copies(turn)
         each(group - 1, lambda k: plane(k).wait_send())
         each(n_lev - 1, lambda k: column(k).wait_send())
@@ -523,6 +558,9 @@
             pltpu.VMEM((2, 2, 8, lanes), f32),
             pltpu.VMEM((2, group, 8, lanes), f32),
             pltpu.VMEM((2, n_lev, 8, lanes), f32),
+            pltpu.VMEM((min(32, n_lev * group), 8, lanes), f32),
+            dma((min(32, n_lev * group),)),
+            dma((min(32, n_lev * group),)),
             dma((passes, PARTS, 3, 2)),
             dma((passes, PARTS, 3, 2)),
             dma((2, group)),

time: 54.5 us -> 54.1 us (level)
  no operation moved by 1% of the time
where the time goes in v4:
time: 54.1 us; the launch traced here: 53.8 us
  Pallas kernels  50.5 us (93%)
  other arithmetic  1.93 us (4%)
  between operations  0.7 us (1%)
  local copies, waits for them, and re-layouts  0.65 us (1%)
    pallas_call x1, Pallas kernels, body(): pl.pallas_call(functools.partial(kernel, sizes), out_shape=[jax.ShapeDtyp...  50.5 us
    add x1, other arithmetic, body(): new_residual + ratio * direction  1.93 us

profile of v4, /device:TPU:0, one launch (start us, length us, event | category | flops | bytes accessed | tf_op | source)
XLA Modules:
  0.0 53.8 jit_solution(2015474093881563978)
XLA Ops:
  0.6 0.0 copy-start
  0.6 0.0 copy-start.1
  0.7 0.0 copy-start.2
  0.7 50.5 %cg_step.1 = (f32[36,2,8,128]{3,2,1,0:T(8,128)}, f32[8,128]{1,0:T(8,128)}, f32[8,128]{1,0:T(8,128)}) custom-call(f32[36,2,8,128]{3,2,1,0:T(8,128)} %direction_hbm.1, f32[36,2,8,128]{3,2,1,0:T(8,128)} %residual_hbm.1, bf16[32,4,2,8,128]{4,3,2,1,0:T(8,128)(2,1)} %ensemble_hbm.1, f32[4,2,8,128]{3,2,1,0:T(8,128)} %static_sd_hbm.1, ...), custom_call_target="tpu_custom_call" | custom-call | flops 100000000 | bytes 3000000 | tf_op jit(solution)/shard_map/cg_step/pallas_call | solution.py:529
  51.2 0.0 copy-start.3
  51.2 0.0 copy-done
  51.2 0.0 copy-done.1
  51.3 0.0 copy-done.2
  51.3 0.6 %copy-done.3 = f32[8,128]{1,0:T(8,128)S(1)} copy-done((f32[8,128]{1,0:T(8,128)S(1)}, f32[8,128]{1,0:T(8,128)}, u32[]{:S(2)}) %copy-start.3) | copy-done | bytes 4120
  51.9 1.9 %multiply_add_fusion = (f32[36,2,8,128]{3,2,1,0:T(8,128)}, f32[36,2,8,128]{3,2,1,0:T(8,128)}, f32[36,2,8,128]{3,2,1,0:T(8,128)}) fusion(f32[36,2,8,128]{3,2,1,0:T(8,128)S(1)} %copy-done, f32[8,128]{1,0:T(8,128)} %get-tuple-element.8, f32[36,2,8,128]{3,2,1,0:T(8,128)S(1)} %copy-done.1, f32[36,2,8,128]{3,2,1,0:T(8,128)} %get-tuple-element.7, ...), kind=kLoop, calls=%fused_computation | loop fusion | flops 442368 | bytes 2072576 | tf_op jit(solution)/shard_map/add | solution.py:592
Async XLA Ops:
  0.6 50.6 %copy-start = (f32[36,2,8,128]{3,2,1,0:T(8,128)S(1)}, f32[36,2,8,128]{3,2,1,0:T(8,128)}, u32[]{:S(2)}) copy-start(f32[36,2,8,128]{3,2,1,0:T(8,128)} %direction_hbm.1) | copy-start | bytes 884740
  0.6 50.6 %copy-start.1 = (f32[36,2,8,128]{3,2,1,0:T(8,128)S(1)}, f32[36,2,8,128]{3,2,1,0:T(8,128)}, u32[]{:S(2)}) copy-start(f32[36,2,8,128]{3,2,1,0:T(8,128)} %residual_hbm.1) | copy-start | bytes 884740
  0.7 50.6 %copy-start.2 = (f32[36,2,8,128]{3,2,1,0:T(8,128)S(1)}, f32[36,2,8,128]{3,2,1,0:T(8,128)}, u32[]{:S(2)}) copy-start(f32[36,2,8,128]{3,2,1,0:T(8,128)} %param.9) | copy-start | bytes 884740
  51.2 0.7 %copy-start.3 = (f32[8,128]{1,0:T(8,128)S(1)}, f32[8,128]{1,0:T(8,128)}, u32[]{:S(2)}) copy-start(f32[8,128]{1,0:T(8,128)} %get-tuple-element.6) | copy-start | bytes 12292
